TPU v7x, 128 devices: a whole 4x4x4 slice. The times are simulated.
128 devices in a mesh: dp: 64 (over x, y, z_hi, core), tensor: 2 (over z_lo).
Axes of the slice: x: 4, y: 4, z: 4 (z_hi: 2, z_lo: 2; z = z_hi * 2 + z_lo), core: 2. Of those that a mesh axis runs over, the one named last changes fastest.
Arguments:
- block_input: bfloat16 [16384, 2048], P(('dp', 'tensor')), may hold values from -24 to 24
- output_grad: bfloat16 [16384, 2048], P(('dp', 'tensor')), may hold values from -24 to 24
- segment_ids: int32 [64, 256], P('dp'), may hold values from 0 to 3, as said below
- norm_gains: float32 [4224], replicated, may hold values from 0.5 to 1.5
- gain_moment: float32 [4224], replicated, may hold values from -240.768 to 240.768
- gain_square: float32 [4224], replicated, may hold values from 5.91872 to 4258.5293
- query_weight: float32 [2048, 2048], P('dp', 'tensor'), may hold values from -0.125 to 0.125
- query_moment: float32 [2048, 2048], P('dp', 'tensor'), may hold values from -80 to 80
- query_square: float32 [2048, 2048], P('dp', 'tensor'), may hold values from 8.192 to 131.072
- key_weight: float32 [2048, 512], P('dp', 'tensor'), may hold values from -0.125 to 0.125
- key_moment: float32 [2048, 512], P('dp', 'tensor'), may hold values from -160 to 160
- key_square: float32 [2048, 512], P('dp', 'tensor'), may hold values from 32.768 to 524.288
- value_weight: float32 [2048, 512], P('dp', 'tensor'), may hold values from -0.125 to 0.125
- value_moment: float32 [2048, 512], P('dp', 'tensor'), may hold values from -256 to 256
- value_square: float32 [2048, 512], P('dp', 'tensor'), may hold values from 73.728 to 1179.648
- output_weight: float32 [2048, 2048], P('dp', 'tensor'), may hold values from -0.75 to 0.75
- output_moment: float32 [2048, 2048], P('dp', 'tensor'), may hold values from -16 to 16
- output_square: float32 [2048, 2048], P('dp', 'tensor'), may hold values from 0.32768 to 5.24288
- gate_weight: float32 [2048, 8192], P('dp', 'tensor'), may hold values from -0.125 to 0.125
- gate_moment: float32 [2048, 8192], P('dp', 'tensor'), may hold values from -24 to 24
- gate_square: float32 [2048, 8192], P('dp', 'tensor'), may hold values from 0.73728 to 11.79648
- up_weight: float32 [2048, 8192], P('dp', 'tensor'), may hold values from -0.125 to 0.125
- up_moment: float32 [2048, 8192], P('dp', 'tensor'), may hold values from -24 to 24
- up_square: float32 [2048, 8192], P('dp', 'tensor'), may hold values from 0.73728 to 11.79648
- down_weight: float32 [2048, 8192], P('dp', 'tensor'), may hold values from -0.0625 to 0.0625
- down_moment: float32 [2048, 8192], P('dp', 'tensor'), may hold values from -48 to 48
- down_square: float32 [2048, 8192], P('dp', 'tensor'), may hold values from 2.94912 to 47.5136
Outputs:
- block_output: float32 [16384, 2048], P(('dp', 'tensor'))
- input_grad: float32 [16384, 2048], P(('dp', 'tensor'))
- gains_updated: float32 [4224], replicated
- gain_momentum: float32 [4224], replicated
- gain_variance: float32 [4224], replicated
- query_updated: float32 [2048, 2048], P('dp', 'tensor')
- query_momentum: float32 [2048, 2048], P('dp', 'tensor')
- query_variance: float32 [2048, 2048], P('dp', 'tensor')
- key_updated: float32 [2048, 512], P('dp', 'tensor')
- key_momentum: float32 [2048, 512], P('dp', 'tensor')
- key_variance: float32 [2048, 512], P('dp', 'tensor')
- value_updated: float32 [2048, 512], P('dp', 'tensor')
- value_momentum: float32 [2048, 512], P('dp', 'tensor')
- value_variance: float32 [2048, 512], P('dp', 'tensor')
- output_updated: float32 [2048, 2048], P('dp', 'tensor')
- output_momentum: float32 [2048, 2048], P('dp', 'tensor')
- output_variance: float32 [2048, 2048], P('dp', 'tensor')
- gate_updated: float32 [2048, 8192], P('dp', 'tensor')
- gate_momentum: float32 [2048, 8192], P('dp', 'tensor')
- gate_variance: float32 [2048, 8192], P('dp', 'tensor')
- up_updated: float32 [2048, 8192], P('dp', 'tensor')
- up_momentum: float32 [2048, 8192], P('dp', 'tensor')
- up_variance: float32 [2048, 8192], P('dp', 'tensor')
- down_updated: float32 [2048, 8192], P('dp', 'tensor')
- down_momentum: float32 [2048, 8192], P('dp', 'tensor')
- down_variance: float32 [2048, 8192], P('dp', 'tensor')
Inputs may be any that keep to these rules, and one draw needn't show every extreme that they name: `segment_ids`: ids never fall along a row; the document holding position 128 begins before 256 // 4 and ends at or after 3 * 64 - 1.
All inputs are finite; a program needn't handle non-finite values.
Results may differ from a plain program's by a relative error of at most 0.015.
Values may be sent and summed in bfloat16 or wider, within the bound.
A program may use at most 320 MiB of HBM per device.

v0:
```python
import jax
import jax.numpy as jnp
from jax import lax
from jax.sharding import PartitionSpec as P

D = 2048
HD = 64
STEP = 10


epsilon = 1e-06
rope_base = 1000000.0
beta_one = 0.9
beta_two = 0.999
adam_epsilon = 1e-08
weight_decay = 0.1
matrix_rates = (0.04, 0.04, 0.04, 0.15, 0.04, 0.04, 0.02)
gain_rate = 0.3
masked_score = -1000000000.0


def rows_product(left, right):
    return lax.dot_general(
        left, right, (((0,), (0,)), ((), ())), preferred_element_type=jnp.float32
    )


def column_product(left, right):
    return lax.dot_general(
        left, right, (((1,), (1,)), ((), ())), preferred_element_type=jnp.float32
    )


def norm_forward(values, gain):
    inverse = lax.rsqrt(jnp.mean(values * values, axis=-1, keepdims=True) + epsilon)
    return (values * inverse * gain, inverse)


def norm_backward(values, inverse, gain, upstream):
    scaled = upstream * gain
    inner = jnp.mean(values * scaled, axis=-1, keepdims=True)
    return (inverse * (scaled - values * inverse * inverse * inner), upstream * values * inverse)


def positions_of(segment_row):
    places = jnp.arange(segment_row.shape[0], dtype=jnp.int32)
    fresh = jnp.concatenate([jnp.ones((1,), dtype=jnp.bool_), segment_row[1:] != segment_row[:-1]])
    starts = jnp.where(fresh, places, jnp.zeros_like(places))
    return places - lax.cummax(starts, axis=0)


def rope_tables(positions):
    half_dim = HD // 2
    frequency = rope_base ** (-2.0 * jnp.arange(half_dim, dtype=jnp.float32) / HD)
    angles = positions.astype(jnp.float32)[:, None] * frequency[None, :]
    return (jnp.cos(angles), jnp.sin(angles))


def rotate(values, cosine, sine):
    half_dim = HD // 2
    front_half = values[..., :half_dim]
    back_half = values[..., half_dim:]
    cos_wide = cosine[:, None, :]
    sin_wide = sine[:, None, :]
    return jnp.concatenate(
        [
            front_half * cos_wide - back_half * sin_wide,
            back_half * cos_wide + front_half * sin_wide,
        ],
        axis=-1,
    )


def unrotate(values, cosine, sine):
    half_dim = HD // 2
    front_half = values[..., :half_dim]
    back_half = values[..., half_dim:]
    cos_wide = cosine[:, None, :]
    sin_wide = sine[:, None, :]
    return jnp.concatenate(
        [
            front_half * cos_wide + back_half * sin_wide,
            back_half * cos_wide - front_half * sin_wide,
        ],
        axis=-1,
    )


def adam_step(weights_now, moment_now, square_now, gradient, step_rate, decay_rate):
    momentum = beta_one * moment_now + (1.0 - beta_one) * gradient
    variance = beta_two * square_now + (1.0 - beta_two) * gradient * gradient
    ratio = (
        momentum
        / (1.0 - beta_one**STEP)
        / (jnp.sqrt(variance / (1.0 - beta_two**STEP)) + adam_epsilon)
    )
    return (weights_now - step_rate * (ratio + decay_rate * weights_now), momentum, variance)


def local(
    block_input,
    output_grad,
    segment_ids,
    norm_gains,
    gain_moment,
    gain_square,
    query_weight,
    query_moment,
    query_square,
    key_weight,
    key_moment,
    key_square,
    value_weight,
    value_moment,
    value_square,
    output_weight,
    output_moment,
    output_square,
    gate_weight,
    gate_moment,
    gate_square,
    up_weight,
    up_moment,
    up_square,
    down_weight,
    down_moment,
    down_square,
):
    query_full, key_full, value_full, output_full, gate_full, up_full, down_full = (
        lax.all_gather(query_weight.astype(jnp.bfloat16), "dp", axis=0, tiled=True),
        lax.all_gather(key_weight.astype(jnp.bfloat16), "dp", axis=0, tiled=True),
        lax.all_gather(value_weight.astype(jnp.bfloat16), "dp", axis=0, tiled=True),
        lax.all_gather(output_weight.astype(jnp.bfloat16), "dp", axis=0, tiled=True),
        lax.all_gather(gate_weight.astype(jnp.bfloat16), "dp", axis=0, tiled=True),
        lax.all_gather(up_weight.astype(jnp.bfloat16), "dp", axis=0, tiled=True),
        lax.all_gather(down_weight.astype(jnp.bfloat16), "dp", axis=0, tiled=True),
    )
    gain_one = norm_gains[:D]
    gain_two = norm_gains[D : 2 * D]
    gain_query = norm_gains[2 * D : 2 * D + HD]
    gain_key = norm_gains[2 * D + HD :]
    seq_len = segment_ids.shape[1]
    heads_local = query_full.shape[1] // HD
    kv_local = key_full.shape[1] // HD
    group_size = heads_local // kv_local
    score_scale = HD ** (-0.5)
    rows_in = block_input.astype(jnp.float32)
    normed_one, inverse_one = norm_forward(rows_in, gain_one)
    gathered_one = lax.all_gather(normed_one.astype(jnp.bfloat16), "tensor", axis=0, tiled=True)
    query_pre = jnp.dot(gathered_one, query_full, preferred_element_type=jnp.float32).reshape(
        seq_len, heads_local, HD
    )
    key_pre = jnp.dot(gathered_one, key_full, preferred_element_type=jnp.float32).reshape(
        seq_len, kv_local, HD
    )
    value_low = (
        jnp.dot(gathered_one, value_full, preferred_element_type=jnp.float32)
        .astype(jnp.bfloat16)
        .reshape(seq_len, kv_local, HD)
    )
    segment_row = segment_ids[0]
    cosine, sine = rope_tables(positions_of(segment_row))
    query_normed, query_inverse = norm_forward(query_pre, gain_query)
    key_normed, key_inverse = norm_forward(key_pre, gain_key)
    query_rot = (
        rotate(query_normed, cosine, sine)
        .astype(jnp.bfloat16)
        .reshape(seq_len, kv_local, group_size, HD)
    )
    key_rot = rotate(key_normed, cosine, sine).astype(jnp.bfloat16)
    places = jnp.arange(seq_len, dtype=jnp.int32)
    allowed = (segment_row[:, None] == segment_row[None, :]) & (places[None, :] <= places[:, None])

    def masked_scores():
        raw = (
            jnp.einsum("qgjd,kgd->gjqk", query_rot, key_rot, preferred_element_type=jnp.float32)
            * score_scale
        )
        return jnp.where(allowed, raw, masked_score)

    scores = masked_scores()
    top_score = jnp.max(scores, axis=-1, keepdims=True)
    exps_now = jnp.exp(scores - top_score)
    totals = jnp.sum(exps_now, axis=-1, keepdims=True)
    probs_low = (exps_now / totals).astype(jnp.bfloat16)
    log_total = top_score + jnp.log(totals)
    attended = jnp.einsum(
        "gjqk,kgd->qgjd", probs_low, value_low, preferred_element_type=jnp.float32
    )
    mixed_low = attended.reshape(seq_len, heads_local * HD).astype(jnp.bfloat16)
    middle = rows_in + lax.psum_scatter(
        column_product(mixed_low, output_full).astype(jnp.bfloat16),
        "tensor",
        scatter_dimension=0,
        tiled=True,
    ).astype(jnp.float32)
    normed_two, inverse_two = norm_forward(middle, gain_two)
    gathered_two = lax.all_gather(normed_two.astype(jnp.bfloat16), "tensor", axis=0, tiled=True)
    gate_pre = jnp.dot(gathered_two, gate_full, preferred_element_type=jnp.float32)
    up_pre = jnp.dot(gathered_two, up_full, preferred_element_type=jnp.float32)
    sigmoid_gate = jax.nn.sigmoid(gate_pre)
    silu_gate = gate_pre * sigmoid_gate
    hidden_low = (silu_gate * up_pre).astype(jnp.bfloat16)
    block_output = middle + lax.psum_scatter(
        column_product(hidden_low, down_full).astype(jnp.bfloat16),
        "tensor",
        scatter_dimension=0,
        tiled=True,
    ).astype(jnp.float32)
    gathered_cot = lax.all_gather(output_grad, "tensor", axis=0, tiled=True)
    hidden_grad = jnp.dot(gathered_cot, down_full, preferred_element_type=jnp.float32)
    down_grad = rows_product(gathered_cot, hidden_low)
    up_low_grad = (hidden_grad * silu_gate).astype(jnp.bfloat16)
    gate_low_grad = (
        hidden_grad * up_pre * (sigmoid_gate + gate_pre * sigmoid_gate * (1.0 - sigmoid_gate))
    ).astype(jnp.bfloat16)
    gate_grad = rows_product(gathered_two, gate_low_grad)
    up_grad = rows_product(gathered_two, up_low_grad)
    normed_two_grad = lax.psum_scatter(
        (column_product(gate_low_grad, gate_full) + column_product(up_low_grad, up_full)).astype(
            jnp.bfloat16
        ),
        "tensor",
        scatter_dimension=0,
        tiled=True,
    ).astype(jnp.float32)
    middle_back, gain_two_terms = norm_backward(middle, inverse_two, gain_two, normed_two_grad)
    middle_grad = output_grad.astype(jnp.float32) + middle_back
    gathered_attn = lax.all_gather(middle_grad.astype(jnp.bfloat16), "tensor", axis=0, tiled=True)
    output_grad_local = rows_product(gathered_attn, mixed_low)
    mixed_grad = (
        jnp.dot(gathered_attn, output_full, preferred_element_type=jnp.float32)
        .astype(jnp.bfloat16)
        .reshape(seq_len, kv_local, group_size, HD)
    )
    probs = jnp.exp(masked_scores() - log_total)
    probs_again = probs.astype(jnp.bfloat16)
    prob_grad = jnp.einsum(
        "qgjd,kgd->gjqk", mixed_grad, value_low, preferred_element_type=jnp.float32
    )
    inner_term = jnp.sum(probs * prob_grad, axis=-1, keepdims=True)
    score_grad = (probs * (prob_grad - inner_term)).astype(jnp.bfloat16)
    query_rot_grad = (
        jnp.einsum(
            "gjqk,kgd->qgjd", score_grad, key_rot, preferred_element_type=jnp.float32
        ).reshape(seq_len, heads_local, HD)
        * score_scale
    )
    key_rot_grad = (
        jnp.einsum("gjqk,qgjd->kgd", score_grad, query_rot, preferred_element_type=jnp.float32)
        * score_scale
    )
    value_low_grad = (
        jnp.einsum("gjqk,qgjd->kgd", probs_again, mixed_grad, preferred_element_type=jnp.float32)
        .reshape(seq_len, kv_local * HD)
        .astype(jnp.bfloat16)
    )
    query_pre_grad, gain_query_terms = norm_backward(
        query_pre, query_inverse, gain_query, unrotate(query_rot_grad, cosine, sine)
    )
    key_pre_grad, gain_key_terms = norm_backward(
        key_pre, key_inverse, gain_key, unrotate(key_rot_grad, cosine, sine)
    )
    query_low_grad = query_pre_grad.reshape(seq_len, heads_local * HD).astype(jnp.bfloat16)
    key_low_grad = key_pre_grad.reshape(seq_len, kv_local * HD).astype(jnp.bfloat16)
    query_grad = rows_product(gathered_one, query_low_grad)
    key_grad = rows_product(gathered_one, key_low_grad)
    value_grad = rows_product(gathered_one, value_low_grad)
    normed_one_grad = lax.psum_scatter(
        (
            column_product(query_low_grad, query_full)
            + column_product(key_low_grad, key_full)
            + column_product(value_low_grad, value_full)
        ).astype(jnp.bfloat16),
        "tensor",
        scatter_dimension=0,
        tiled=True,
    ).astype(jnp.float32)
    input_back, gain_one_terms = norm_backward(rows_in, inverse_one, gain_one, normed_one_grad)
    input_grad = middle_grad + input_back
    gain_local = jnp.concatenate(
        [
            jnp.sum(gain_one_terms, axis=0),
            jnp.sum(gain_two_terms, axis=0),
            jnp.sum(gain_query_terms, axis=(0, 1)),
            jnp.sum(gain_key_terms, axis=(0, 1)),
        ]
    )
    gain_grads = lax.psum(gain_local, ("dp", "tensor"))
    query_summed, key_summed, value_summed, output_summed, gate_summed, up_summed, down_summed = (
        lax.psum_scatter(query_grad, "dp", scatter_dimension=0, tiled=True),
        lax.psum_scatter(key_grad, "dp", scatter_dimension=0, tiled=True),
        lax.psum_scatter(value_grad, "dp", scatter_dimension=0, tiled=True),
        lax.psum_scatter(output_grad_local, "dp", scatter_dimension=0, tiled=True),
        lax.psum_scatter(gate_grad, "dp", scatter_dimension=0, tiled=True),
        lax.psum_scatter(up_grad, "dp", scatter_dimension=0, tiled=True),
        lax.psum_scatter(down_grad, "dp", scatter_dimension=0, tiled=True),
    )
    gains_updated, gain_momentum, gain_variance = adam_step(
        norm_gains, gain_moment, gain_square, gain_grads, gain_rate, 0.0
    )
    query_updated, query_momentum, query_variance = adam_step(
        query_weight, query_moment, query_square, query_summed, matrix_rates[0], weight_decay
    )
    key_updated, key_momentum, key_variance = adam_step(
        key_weight, key_moment, key_square, key_summed, matrix_rates[1], weight_decay
    )
    value_updated, value_momentum, value_variance = adam_step(
        value_weight, value_moment, value_square, value_summed, matrix_rates[2], weight_decay
    )
    output_updated, output_momentum, output_variance = adam_step(
        output_weight, output_moment, output_square, output_summed, matrix_rates[3], weight_decay
    )
    gate_updated, gate_momentum, gate_variance = adam_step(
        gate_weight, gate_moment, gate_square, gate_summed, matrix_rates[4], weight_decay
    )
    up_updated, up_momentum, up_variance = adam_step(
        up_weight, up_moment, up_square, up_summed, matrix_rates[5], weight_decay
    )
    down_updated, down_momentum, down_variance = adam_step(
        down_weight, down_moment, down_square, down_summed, matrix_rates[6], weight_decay
    )
    return (
        block_output,
        input_grad,
        gains_updated,
        gain_momentum,
        gain_variance,
        query_updated,
        query_momentum,
        query_variance,
        key_updated,
        key_momentum,
        key_variance,
        value_updated,
        value_momentum,
        value_variance,
        output_updated,
        output_momentum,
        output_variance,
        gate_updated,
        gate_momentum,
        gate_variance,
        up_updated,
        up_momentum,
        up_variance,
        down_updated,
        down_momentum,
        down_variance,
    )


def solution(mesh):
    in_specs = (
        P(("dp", "tensor"), None),
        P(("dp", "tensor"), None),
        P("dp", None),
        P(),
        P(),
        P(),
        P("dp", "tensor"),
        P("dp", "tensor"),
        P("dp", "tensor"),
        P("dp", "tensor"),
        P("dp", "tensor"),
        P("dp", "tensor"),
        P("dp", "tensor"),
        P("dp", "tensor"),
        P("dp", "tensor"),
        P("dp", "tensor"),
        P("dp", "tensor"),
        P("dp", "tensor"),
        P("dp", "tensor"),
        P("dp", "tensor"),
        P("dp", "tensor"),
        P("dp", "tensor"),
        P("dp", "tensor"),
        P("dp", "tensor"),
        P("dp", "tensor"),
        P("dp", "tensor"),
        P("dp", "tensor"),
    )
    out_specs = (
        P(("dp", "tensor"), None),
        P(("dp", "tensor"), None),
        P(),
        P(),
        P(),
        P("dp", "tensor"),
        P("dp", "tensor"),
        P("dp", "tensor"),
        P("dp", "tensor"),
        P("dp", "tensor"),
        P("dp", "tensor"),
        P("dp", "tensor"),
        P("dp", "tensor"),
        P("dp", "tensor"),
        P("dp", "tensor"),
        P("dp", "tensor"),
        P("dp", "tensor"),
        P("dp", "tensor"),
        P("dp", "tensor"),
        P("dp", "tensor"),
        P("dp", "tensor"),
        P("dp", "tensor"),
        P("dp", "tensor"),
        P("dp", "tensor"),
        P("dp", "tensor"),
        P("dp", "tensor"),
    )
    return jax.shard_map(local, mesh=mesh, in_specs=in_specs, out_specs=out_specs, check_vma=False)
```

profile of v0, /device:TPU:1, one launch (start us, length us, event | category | flops | bytes accessed | tf_op | source)
XLA Modules:
  0.0 3443.3 jit_solution(15420078006532795107)
XLA Ops:
  9.2 2.0 fusion.26
  14.2 1.5 convert_element_type.124
  15.8 1.5 convert_element_type.129
  20.9 17.6 all-gather.12.cloned.1.call-done
  38.5 71.1 %all-gather.16.cloned.1.call-done = bf16[2048,256]{1,0:T(8,128)(2,1)} async-done(((bf16[32,256]{1,0:T(8,128)(2,1)}), bf16[2048,256]{1,0:T(8,128)(2,1)}) %all-gather.16.cloned.1.call-update) | async-done | bytes 1048592 | tf_op jit(solution)/shard_map/all_gather | solution.py:131
  109.6 2.1 multiply_reduce_fusion.5
  112.3 63.7 %all-gather.14.cloned.1.call-done = bf16[2048,256]{1,0:T(8,128)(2,1)} async-done(((bf16[32,256]{1,0:T(8,128)(2,1)}), bf16[2048,256]{1,0:T(8,128)(2,1)}) %all-gather.14.cloned.1.call-update) | async-done | bytes 1048592 | tf_op jit(solution)/shard_map/all_gather | solution.py:132
  176.1 2.1 convolution_convert_fusion.3
  178.1 71.4 %all-gather.18.cloned.1.call-done = bf16[2048,1024]{1,0:T(8,128)(2,1)} async-done(((bf16[32,1024]{1,0:T(8,128)(2,1)}), bf16[2048,1024]{1,0:T(8,128)(2,1)}) %all-gather.18.cloned.1.call-update) | async-done | bytes 4194320 | tf_op jit(solution)/shard_map/all_gather | solution.py:130
  249.6 4.4 fusion.73
  254.0 1.6 copy.80
  258.9 1.7 fusion.12
  260.6 62.5 %all-gather.20.cloned.1.call-done = bf16[2048,1024]{1,0:T(8,128)(2,1)} async-done(((bf16[32,1024]{1,0:T(8,128)(2,1)}), bf16[2048,1024]{1,0:T(8,128)(2,1)}) %all-gather.20.cloned.1.call-update) | async-done | bytes 4194320 | tf_op jit(solution)/shard_map/all_gather | solution.py:133
  323.1 4.7 convolution_convert_fusion.1
  327.8 19.3 reduce-scatter.12.cloned.1.call-done
  348.5 2.0 multiply_convert_fusion.3
  351.4 1.8 convert_element_type.134
  353.8 1.8 convert_element_type.136
  355.9 19.7 all-gather.22.cloned.1.call-done
  375.6 111.9 %all-gather.24.cloned.1.call-done = bf16[2048,4096]{1,0:T(8,128)(2,1)} async-done(((bf16[32,4096]{1,0:T(8,128)(2,1)}), bf16[2048,4096]{1,0:T(8,128)(2,1)}) %all-gather.24.cloned.1.call-update) | async-done | bytes 16777232 | tf_op jit(solution)/shard_map/all_gather | solution.py:134
  487.5 12.6 fusion.74
  500.1 95.6 %all-gather.26.cloned.1.call-done = bf16[2048,4096]{1,0:T(8,128)(2,1)} async-done(((bf16[32,4096]{1,0:T(8,128)(2,1)}), bf16[2048,4096]{1,0:T(8,128)(2,1)}) %all-gather.26.cloned.1.call-update) | async-done | bytes 16777232 | tf_op jit(solution)/shard_map/all_gather | solution.py:135
  595.6 12.6 fusion.75
  608.2 10.1 all-gather.30.cloned.1.call-done
  618.3 111.9 %all-gather.28.cloned.1.call-done = bf16[2048,4096]{1,0:T(8,128)(2,1)} async-done(((bf16[32,4096]{1,0:T(8,128)(2,1)}), bf16[2048,4096]{1,0:T(8,128)(2,1)}) %all-gather.28.cloned.1.call-update) | async-done | bytes 16777232 | tf_op jit(solution)/shard_map/all_gather | solution.py:136
  730.3 13.5 multiply_convert_fusion
  743.8 12.3 fusion.76
  756.1 12.5 fusion.6
  768.6 20.2 reduce-scatter.16.cloned.1.call-done
  788.8 2.0 fusion.34
  791.4 2.5 fusion.61
  796.1 1.8 mul.681
  797.8 2.5 copy.88
  801.1 17.8 all-gather.32.cloned.1.call-done
  818.9 4.6 convolution_convert_fusion.2
  823.5 2.0 copy.82
  825.5 3.4 fusion
  834.3 2.6 copy.84
  841.3 2.7 multiply_reduce_fusion
  846.5 1.5 fusion.7
  848.3 11.9 convolution_convert_fusion
  860.3 1.8 fusion.79
  862.2 1.8 fusion.80
  864.1 4.6 fusion.78
  870.0 4.5 fusion.81
  875.8 15.1 fusion.82
  891.3 14.8 fusion.83
  907.3 14.9 convolution_bitcast_fusion
  923.4 2.1 fusion.42
  926.9 67.2 %psum.7 = f32[4224]{0:T(1024)} all-reduce(f32[4224]{0:T(1024)} %concatenate.41), channel_id=1, replica_groups=mesh['dp'=64,'tensor'=2] {'dp','tensor'}, use_global_device_ids=true, to_apply=%region_23.24 | all-reduce | flops 4224 | bytes 33792 | tf_op jit(solution)/shard_map/psum | solution.py:289
  996.6 3.5 fusion.29
  1000.1 229.8 %reduce-scatter.22.cloned.1.call-done = f32[32,256]{1,0:T(8,128)} async-done(((f32[2048,256]{1,0:T(8,128)}), f32[32,256]{1,0:T(8,128)}) %reduce-scatter.22.cloned.1.call-update) | async-done | bytes 32784 | tf_op jit(solution)/shard_map/reduce_scatter | solution.py:292
  1230.0 1.5 multiply_subtract_fusion.8
  1231.4 330.1 %reduce-scatter.24.cloned.1.call-done = f32[32,256]{1,0:T(8,128)} async-done(((f32[2048,256]{1,0:T(8,128)}), f32[32,256]{1,0:T(8,128)}) %reduce-scatter.24.cloned.1.call-update) | async-done | bytes 32784 | tf_op jit(solution)/shard_map/reduce_scatter | solution.py:293
  1563.0 342.8 %reduce-scatter.20.cloned.1.call-done = f32[32,1024]{1,0:T(8,128)} async-done(((f32[2048,1024]{1,0:T(8,128)}), f32[32,1024]{1,0:T(8,128)}) %reduce-scatter.20.cloned.1.call-update) | async-done | bytes 131088 | tf_op jit(solution)/shard_map/reduce_scatter | solution.py:291
  1905.8 1.8 multiply_subtract_fusion.5
  1907.6 341.4 %reduce-scatter.26.cloned.1.call-done = f32[32,1024]{1,0:T(8,128)} async-done(((f32[2048,1024]{1,0:T(8,128)}), f32[32,1024]{1,0:T(8,128)}) %reduce-scatter.26.cloned.1.call-update) | async-done | bytes 131088 | tf_op jit(solution)/shard_map/reduce_scatter | solution.py:294
  2249.0 1.8 multiply_subtract_fusion.4
  2250.8 392.3 %reduce-scatter.28.cloned.1.call-done = f32[32,4096]{1,0:T(8,128)} async-done(((f32[2048,4096]{1,0:T(8,128)}), f32[32,4096]{1,0:T(8,128)}) %reduce-scatter.28.cloned.1.call-update) | async-done | bytes 524304 | tf_op jit(solution)/shard_map/reduce_scatter | solution.py:295
  2643.2 2.6 multiply_subtract_fusion.2
  2645.8 392.4 %reduce-scatter.30.cloned.1.call-done = f32[32,4096]{1,0:T(8,128)} async-done(((f32[2048,4096]{1,0:T(8,128)}), f32[32,4096]{1,0:T(8,128)}) %reduce-scatter.30.cloned.1.call-update) | async-done | bytes 524304 | tf_op jit(solution)/shard_map/reduce_scatter | solution.py:296
  3038.1 2.4 multiply_subtract_fusion.1
  3040.6 392.7 %reduce-scatter.32.cloned.1.call-done = f32[32,4096]{1,0:T(8,128)} async-done(((f32[2048,4096]{1,0:T(8,128)}), f32[32,4096]{1,0:T(8,128)}) %reduce-scatter.32.cloned.1.call-update) | async-done | bytes 524304 | tf_op jit(solution)/shard_map/reduce_scatter | solution.py:297
  3433.2 2.7 multiply_subtract_fusion
  (205 shorter events, 42.4 us)
Async XLA Ops:
  7.2 31.3 all-gather.12.cloned.1.call-start
  8.0 103.8 %copy-start.38 = (f32[2048]{0:T(1024)}, f32[2048]{0:T(1024)S(1)}, u32[]{:S(2)}) copy-start(f32[2048]{0:T(1024)S(1)} %get-tuple-element.76) | copy-start | bytes 24580
  8.0 782.9 %copy-start.35 = (f32[2048]{0:T(1024)}, f32[2048]{0:T(1024)S(1)}, u32[]{:S(2)}) copy-start(f32[2048]{0:T(1024)S(1)} %get-tuple-element.75) | copy-start | bytes 24580
  9.2 9.1 copy-start.48
  11.3 98.4 %all-gather.16.cloned.1.call-start = ((), (), s32[]{:S(2)}) async-start(), calls=%async_computation.13 | async-start | bytes 1064960 | tf_op jit(solution)/shard_map/all_gather | solution.py:131
  12.7 163.3 %all-gather.14.cloned.1.call-start = ((), (), s32[]{:S(2)}) async-start(), calls=%async_computation.12 | async-start | bytes 1064960 | tf_op jit(solution)/shard_map/all_gather | solution.py:132
  14.2 235.4 %all-gather.18.cloned.1.call-start = ((), (), s32[]{:S(2)}) async-start(), calls=%async_computation.14 | async-start | bytes 4259840 | tf_op jit(solution)/shard_map/all_gather | solution.py:130
  15.8 307.3 %all-gather.20.cloned.1.call-start = ((), (), s32[]{:S(2)}) async-start(), calls=%async_computation.15 | async-start | bytes 4259840 | tf_op jit(solution)/shard_map/all_gather | solution.py:133
  17.4 329.8 %reduce-scatter.12.cloned.1.call-start = ((), (), s32[]{:S(2)}) async-start(), calls=%async_computation.16 | async-start | bytes 1572864 | tf_op jit(solution)/shard_map/reduce_scatter | solution.py:191
  19.8 235.8 %copy-start.46 = (f32[64]{0:T(128)}, f32[64]{0:T(128)S(1)}, u32[]{:S(2)}) copy-start(f32[64]{0:T(128)S(1)} %get-tuple-element.78) | copy-start | bytes 772
  19.8 775.6 %copy-start.45 = (f32[64]{0:T(128)}, f32[64]{0:T(128)S(1)}, u32[]{:S(2)}) copy-start(f32[64]{0:T(128)S(1)} %get-tuple-element.77) | copy-start | bytes 772
  20.0 235.9 %copy-start.21 = (f32[256,32]{0,1:T(8,128)}, f32[256,32]{0,1:T(8,128)S(1)}, u32[]{:S(2)}) copy-start(f32[256,32]{0,1:T(8,128)S(1)} %get-tuple-element.79) | copy-start | bytes 98308
  20.1 235.9 %copy-start.23 = (f32[256,32]{0,1:T(8,128)}, f32[256,32]{0,1:T(8,128)S(1)}, u32[]{:S(2)}) copy-start(f32[256,32]{0,1:T(8,128)S(1)} %get-tuple-element.80) | copy-start | bytes 98308
  38.5 211.0 %copy-start.3 = (bf16[256,2048]{1,0:T(8,128)(2,1)S(1)}, bf16[256,2048]{1,0:T(8,128)(2,1)}, u32[]{:S(2)}) copy-start(bf16[256,2048]{1,0:T(8,128)(2,1)} %all-gather.12.cloned.1.call-done) | copy-start | bytes 3145732
  112.3 143.8 %copy-start.31 = (bf16[256,4,32]{0,2,1:T(8,128)(2,1)}, bf16[256,4,32]{0,2,1:T(8,128)(2,1)S(1)}, u32[]{:S(2)}) copy-start(bf16[256,4,32]{0,2,1:T(8,128)(2,1)S(1)} %get-tuple-element.71) | copy-start | bytes 196612
  112.3 143.8 %copy-start.33 = (bf16[256,4,32]{0,2,1:T(8,128)(2,1)}, bf16[256,4,32]{0,2,1:T(8,128)(2,1)S(1)}, u32[]{:S(2)}) copy-start(bf16[256,4,32]{0,2,1:T(8,128)(2,1)S(1)} %get-tuple-element.72) | copy-start | bytes 196612
  255.7 1.3 copy-start.37
  256.1 1.5 copy-start.17
  256.1 1.5 copy-start.19
  257.0 2.0 copy-start
  257.0 3.6 copy-start.41
  257.6 3.0 copy-start.42
  260.6 86.6 %copy-start.2 = (bf16[128,2048]{1,0:T(8,128)(2,1)S(1)}, bf16[128,2048]{1,0:T(8,128)(2,1)}, u32[]{:S(2)}) copy-start(bf16[128,2048]{1,0:T(8,128)(2,1)} %param.27) | copy-start | bytes 1572868
  323.1 27.5 copy-start.11
  327.8 47.8 %all-gather.22.cloned.1.call-start = ((), (), s32[]{:S(2)}) async-start(), calls=%async_computation.17 | async-start | bytes 1572864 | tf_op jit(solution)/shard_map/all_gather | solution.py:198
  348.5 442.4 %copy-start.44 = (f32[128]{0:T(128)}, f32[128]{0:T(128)S(1)}, u32[]{:S(2)}) copy-start(f32[128]{0:T(128)S(1)} %add_rsqrt_fusion.2) | copy-start | bytes 1540
  350.5 136.9 %all-gather.24.cloned.1.call-start = ((), (), s32[]{:S(2)}) async-start(), calls=%async_computation.18 | async-start | bytes 17039360 | tf_op jit(solution)/shard_map/all_gather | solution.py:134
  351.3 244.3 %all-gather.26.cloned.1.call-start = ((), (), s32[]{:S(2)}) async-start(), calls=%async_computation.19 | async-start | bytes 17039360 | tf_op jit(solution)/shard_map/all_gather | solution.py:135
  353.2 265.1 %all-gather.30.cloned.1.call-start = ((), (), s32[]{:S(2)}) async-start(), calls=%async_computation.22 | async-start | bytes 1572864 | tf_op jit(solution)/shard_map/all_gather | solution.py:210
  353.8 376.5 %all-gather.28.cloned.1.call-start = ((), (), s32[]{:S(2)}) async-start(), calls=%async_computation.20 | async-start | bytes 17039360 | tf_op jit(solution)/shard_map/all_gather | solution.py:136
  355.6 433.2 %reduce-scatter.16.cloned.1.call-start = ((), (), s32[]{:S(2)}) async-start(), calls=%async_computation.23 | async-start | bytes 1572864 | tf_op jit(solution)/shard_map/reduce_scatter | solution.py:219
  756.1 32.8 copy-start.4
  768.6 50.3 %all-gather.32.cloned.1.call-start = ((), (), s32[]{:S(2)}) async-start(), calls=%async_computation.24 | async-start | bytes 1572864 | tf_op jit(solution)/shard_map/all_gather | solution.py:229
  793.9 129.6 %reduce-scatter.18.cloned.1.call-start = ((), (), s32[]{:S(2)}) async-start(), calls=%async_computation.25 | async-start | bytes 1572864 | tf_op jit(solution)/shard_map/reduce_scatter | solution.py:269
  825.5 3.6 copy-start.1
  829.1 1.6 copy-start.18
  829.1 1.6 copy-start.20
  830.2 2.0 copy-start.7
  830.7 2.3 copy-start.22
  830.7 2.3 copy-start.24
  838.2 5.8 copy-start.50
  844.0 1.3 copy-start.9
  848.0 148.6 %reduce-scatter.14.cloned.1.call-start = ((), (), s32[]{:S(2)}) async-start(), calls=%async_computation.21 | async-start | bytes 1572864 | tf_op jit(solution)/shard_map/reduce_scatter | solution.py:204
  860.2 369.8 %reduce-scatter.22.cloned.1.call-start = ((), (), s32[]{:S(2)}) async-start(), calls=%async_computation.27 | async-start | bytes 2129920 | tf_op jit(solution)/shard_map/reduce_scatter | solution.py:292
  862.1 699.4 %reduce-scatter.24.cloned.1.call-start = ((), (), s32[]{:S(2)}) async-start(), calls=%async_computation.28 | async-start | bytes 2129920 | tf_op jit(solution)/shard_map/reduce_scatter | solution.py:293
  864.0 1041.8 %reduce-scatter.20.cloned.1.call-start = ((), (), s32[]{:S(2)}) async-start(), calls=%async_computation.26 | async-start | bytes 8519680 | tf_op jit(solution)/shard_map/reduce_scatter | solution.py:291
  868.7 1.4 copy-start.28
  868.7 1380.3 %reduce-scatter.26.cloned.1.call-start = ((), (), s32[]{:S(2)}) async-start(), calls=%async_computation.29 | async-start | bytes 8519680 | tf_op jit(solution)/shard_map/reduce_scatter | solution.py:294
  874.6 1768.6 %reduce-scatter.28.cloned.1.call-start = ((), (), s32[]{:S(2)}) async-start(), calls=%async_computation.30 | async-start | bytes 34078720 | tf_op jit(solution)/shard_map/reduce_scatter | solution.py:295
  891.0 2147.2 %reduce-scatter.30.cloned.1.call-start = ((), (), s32[]{:S(2)}) async-start(), calls=%async_computation.31 | async-start | bytes 34078720 | tf_op jit(solution)/shard_map/reduce_scatter | solution.py:296
  906.1 2527.2 %reduce-scatter.32.cloned.1.call-start = ((), (), s32[]{:S(2)}) async-start(), calls=%async_computation.32 | async-start | bytes 34078720 | tf_op jit(solution)/shard_map/reduce_scatter | solution.py:297
  922.1 1.3 copy-start.39
  922.1 74.5 %copy-start.6 = (bf16[128,2048]{1,0:T(8,128)(2,1)S(1)}, bf16[128,2048]{1,0:T(8,128)(2,1)}, u32[]{:S(2)}) copy-start(bf16[128,2048]{1,0:T(8,128)(2,1)} %param.28) | copy-start | bytes 1572868
  922.1 74.5 %copy-start.8 = (bf16[128,2048]{1,0:T(8,128)(2,1)S(1)}, bf16[128,2048]{1,0:T(8,128)(2,1)}, u32[]{:S(2)}) copy-start(bf16[128,2048]{1,0:T(8,128)(2,1)} %reduce-scatter.16.cloned.1.call-done) | copy-start | bytes 1572868
  922.1 74.5 %copy-start.36 = (f32[2048]{0:T(1024)S(1)}, f32[2048]{0:T(1024)}, u32[]{:S(2)}) copy-start(f32[2048]{0:T(1024)} %copy-done.35) | copy-start | bytes 24580
  922.2 983.6 %copy-start.29 = (f32[32,1024]{1,0:T(8,128)S(1)}, f32[32,1024]{1,0:T(8,128)}, u32[]{:S(2)}) copy-start(f32[32,1024]{1,0:T(8,128)} %param.33) | copy-start | bytes 393220
  922.2 983.6 %copy-start.40 = (f32[32,1024]{1,0:T(8,128)S(1)}, f32[32,1024]{1,0:T(8,128)}, u32[]{:S(2)}) copy-start(f32[32,1024]{1,0:T(8,128)} %param.34) | copy-start | bytes 393220
  922.2 1326.8 %copy-start.30 = (f32[32,1024]{1,0:T(8,128)S(1)}, f32[32,1024]{1,0:T(8,128)}, u32[]{:S(2)}) copy-start(f32[32,1024]{1,0:T(8,128)} %param.42) | copy-start | bytes 393220
  923.4 1719.7 %copy-start.12 = (f32[32,4096]{1,0:T(8,128)S(1)}, f32[32,4096]{1,0:T(8,128)}, u32[]{:S(2)}) copy-start(f32[32,4096]{1,0:T(8,128)} %param.45) | copy-start | bytes 1572868
  923.4 1719.7 %copy-start.25 = (f32[32,4096]{1,0:T(8,128)S(1)}, f32[32,4096]{1,0:T(8,128)}, u32[]{:S(2)}) copy-start(f32[32,4096]{1,0:T(8,128)} %param.46) | copy-start | bytes 1572868
  1000.1 2038.0 %copy-start.13 = (f32[32,4096]{1,0:T(8,128)S(1)}, f32[32,4096]{1,0:T(8,128)}, u32[]{:S(2)}) copy-start(f32[32,4096]{1,0:T(8,128)} %param.48) | copy-start | bytes 1572868
  1000.1 2038.0 %copy-start.26 = (f32[32,4096]{1,0:T(8,128)S(1)}, f32[32,4096]{1,0:T(8,128)}, u32[]{:S(2)}) copy-start(f32[32,4096]{1,0:T(8,128)} %param.49) | copy-start | bytes 1572868
  1000.1 2038.0 %copy-start.27 = (f32[32,4096]{1,0:T(8,128)S(1)}, f32[32,4096]{1,0:T(8,128)}, u32[]{:S(2)}) copy-start(f32[32,4096]{1,0:T(8,128)} %param.50) | copy-start | bytes 1572868
  1907.6 1525.7 %copy-start.14 = (f32[32,4096]{1,0:T(8,128)S(1)}, f32[32,4096]{1,0:T(8,128)}, u32[]{:S(2)}) copy-start(f32[32,4096]{1,0:T(8,128)} %param.51) | copy-start | bytes 1572868
  (9 other events, 9.1 us)
Sparse Core Ops, SparseCore 0:
  11.4 27.1 all-gather.11
  42.2 67.4 all-gather.15
  113.3 62.7 all-gather.13
  179.5 69.9 all-gather.17
  253.0 70.0 all-gather.19
  327.9 19.1 reduce-scatter.11
  350.7 24.8 all-gather.21
  379.6 107.7 all-gather.23
  491.5 104.0 all-gather.25
  597.2 21.0 all-gather.29
  622.4 107.8 all-gather.27
  768.7 20.0 reduce-scatter.15
  794.0 24.8 all-gather.31
  848.2 23.8 reduce-scatter.17
  875.0 23.8 reduce-scatter.13
  901.1 328.8 reduce-scatter.21
  1232.3 329.1 reduce-scatter.23
  1563.8 341.9 reduce-scatter.19
  1908.2 340.7 reduce-scatter.25
  2251.3 391.8 reduce-scatter.27
  2645.6 392.4 reduce-scatter.29
  3040.5 392.6 reduce-scatter.31
where the time goes:
time: 3450 us; the launch traced here: 3440 us
  waiting for transfers between devices  3120 us (90%)
  matrix products  163 us (5%)
  blocking collectives  67.2 us (2%)
  other arithmetic  57 us (2%)
    reduce_scatter x1, waiting for transfers between devices, local(): lax.psum_scatter(down_grad, 'dp', scatter_dimension=0, tiled=True)  393 us
    reduce_scatter x1, waiting for transfers between devices, local(): lax.psum_scatter(up_grad, 'dp', scatter_dimension=0, tiled=True)  392 us
    reduce_scatter x1, waiting for transfers between devices, local(): lax.psum_scatter(gate_grad, 'dp', scatter_dimension=0, tiled=True)  392 us
    reduce_scatter x1, waiting for transfers between devices, local(): lax.psum_scatter(query_grad, 'dp', scatter_dimension=0, tiled=True)  343 us
    reduce_scatter x1, waiting for transfers between devices, local(): lax.psum_scatter(output_grad_local, 'dp', scatter_dimension=0, tiled=True)  341 us
    reduce_scatter x1, waiting for transfers between devices, local(): lax.psum_scatter(value_grad, 'dp', scatter_dimension=0, tiled=True)  330 us
    reduce_scatter x1, waiting for transfers between devices, local(): lax.psum_scatter(key_grad, 'dp', scatter_dimension=0, tiled=True)  230 us
    all_gather x1, waiting for transfers between devices, local(): lax.all_gather(down_weight.astype(jnp.bfloat16), 'dp', axis=0, tiled=True)  112 us
  transfers between devices with their start and end apart: 22, of which 20 were waited for; matrix products, arithmetic and copies ran while one was open for 4% of the time, Pallas kernels for 0%

commit v1 on v0

v1 whole, which is shorter than its diff:
```python
import jax
import jax.numpy as jnp
from jax import lax
from jax.experimental import pallas as pl
from jax.experimental.pallas import tpu as pltpu

MESH = pl.DeviceIdType.MESH
VM = pltpu.VMEM
bf16 = jnp.bfloat16
f32 = jnp.float32


def m4(v):
    return lax.rem(v + 4, 4)


class Place:
    def __init__(self):
        dp = lax.axis_index("dp")
        self.l = lax.axis_index("tensor")
        self.x = lax.div(dp, 16)
        self.y = lax.rem(lax.div(dp, 4), 4)
        self.h = lax.rem(lax.div(dp, 2), 2)
        self.c = lax.rem(dp, 2)
        self.z = self.h * 2 + self.l

    def at(self, x=None, y=None, z=None, c=None):
        x = self.x if x is None else x
        y = self.y if y is None else y
        z = self.z if z is None else z
        c = self.c if c is None else c
        return (x * 16 + y * 4 + lax.div(z, 2) * 2 + c, lax.rem(z, 2))

    def pos(self, axis):
        return {"x": self.x, "y": self.y, "z": self.z}[axis]

    def step(self, axis, d):
        return self.at(**{axis: m4(self.pos(axis) + d)})

    def sibling(self):
        return self.at(c=1 - self.c)


class Wire:
    def __init__(self, send, recv):
        self.send, self.recv, self.n = send, recv, 0
        self.pending = []

    def go(self, src, dst, dev):
        i = self.n
        self.n += 1
        c = pltpu.make_async_remote_copy(
            src_ref=src, dst_ref=dst, send_sem=self.send.at[i], recv_sem=self.recv.at[i],
            device_id=dev, device_id_type=MESH)
        c.start()
        self.pending.append(c)
        return c

    def finish(self):
        for c in self.pending:
            c.wait_send()
        self.pending = []


def meet(devs):
    b = pltpu.get_barrier_semaphore()
    for d in devs:
        pl.semaphore_signal(b, inc=1, device_id=d, device_id_type=MESH)
    pl.semaphore_wait(b, len(devs))


def ring_gather(w, me, axis, whole, lo, hi, first=None, arrived=None):
    p = me.pos(axis)
    up, down = me.step(axis, 1), me.step(axis, -1)
    own = whole(p) if first is None else first
    a = w.go(own, whole(p), up)
    b = w.go(own, whole(p), down)
    yield
    a.wait_recv()
    fa = w.go(lo(m4(p - 1)), lo(m4(p - 1)), up)
    if arrived:
        arrived(whole(m4(p - 1)))
    b.wait_recv()
    fb = w.go(hi(m4(p + 1)), hi(m4(p + 1)), down)
    if arrived:
        arrived(whole(m4(p + 1)))
    yield
    fa.wait_recv()
    if arrived:
        arrived(lo(m4(p - 2)))
    fb.wait_recv()
    if arrived:
        arrived(hi(m4(p - 2)))


def ring_scatter(w, me, axis, lo, hi, tlo, thi, rup, rdown, add):
    p = me.pos(axis)
    up, down = me.step(axis, 1), me.step(axis, -1)
    far, nu, nd = m4(p + 2), m4(p + 1), m4(p - 1)
    ta = w.go(lo(far), tlo, up)
    tb = w.go(hi(far), thi, down)
    da = w.go(hi(nu), rup[1], up)
    db = w.go(lo(nd), rdown[0], down)
    yield
    ta.wait_recv()
    add(tlo, lo(nu))
    sa = w.go(tlo, rup[0], up)
    tb.wait_recv()
    add(thi, hi(nd))
    sb = w.go(thi, rdown[1], down)
    yield
    da.wait_recv()
    db.wait_recv()
    sa.wait_recv()
    sb.wait_recv()


def loop_add(dst, a, b=None, rows=16):
    n = dst.shape[0]

    def body(i, _):
        def inner(j, _):
            s = pl.ds(pl.multiple_of(j * rows, rows), rows)
            v = dst[i, s].astype(f32) + a[i, s].astype(f32)
            if b is not None:
                v = v + b[i, s].astype(f32)
            dst[i, s] = v.astype(dst.dtype)
            return 0
        return lax.fori_loop(0, dst.shape[1] // rows, inner, 0)
    lax.fori_loop(0, n, body, 0)


def run(gens):
    gens = list(gens)
    while gens:
        for g in list(gens):
            try:
                next(g)
            except StopIteration:
                gens.remove(g)


def params(cid, mb=56):
    return pltpu.CompilerParams(collective_id=cid, has_side_effects=True, vmem_limit_bytes=mb * 2**20)


def ag_xy_gens(w, me, src, out):
    H = 64
    x, y = me.x, me.y

    def half_a():
        yield from ring_gather(w, me, "x", lambda i: out.at[i, y, pl.ds(0, 64)], lambda i: out.at[i, y, pl.ds(0, 32)],
                               lambda i: out.at[i, y, pl.ds(32, 32)], first=src.at[pl.ds(0, 64)])
        yield
        yield from ring_gather(w, me, "y", lambda i: out.at[:, i, pl.ds(0, 64)], lambda i: out.at[:, i, pl.ds(0, 32)],
                               lambda i: out.at[:, i, pl.ds(32, 32)])

    def half_b():
        yield from ring_gather(w, me, "y", lambda i: out.at[x, i, pl.ds(64, 64)], lambda i: out.at[x, i, pl.ds(64, 32)],
                               lambda i: out.at[x, i, pl.ds(96, 32)], first=src.at[pl.ds(64, 64)])
        yield
        yield from ring_gather(w, me, "x", lambda i: out.at[i, :, pl.ds(64, 64)], lambda i: out.at[i, :, pl.ds(64, 32)],
                               lambda i: out.at[i, :, pl.ds(96, 32)])
    return [half_a(), half_b()]


def ag_xy(shard, cid, space=pl.ANY):
    C = shard.shape[1]

    def kernel(src, out, send, recv, lsem):
        me = Place()
        meet([me.step("x", 1), me.step("x", -1), me.step("y", 1), me.step("y", -1)])
        w = Wire(send, recv)
        lc = pltpu.make_async_copy(src, out.at[me.x, me.y], lsem)
        lc.start()
        lc.wait()
        run(ag_xy_gens(w, me, src, out))
        w.finish()

    return pl.pallas_call(
        kernel, out_shape=jax.ShapeDtypeStruct((4, 4, 128, C), shard.dtype),
        in_specs=[pl.BlockSpec(memory_space=space)], out_specs=pl.BlockSpec(memory_space=space),
        scratch_shapes=[pltpu.SemaphoreType.DMA((16,)), pltpu.SemaphoreType.DMA((16,)), pltpu.SemaphoreType.DMA],
        compiler_params=params(cid))(shard)


def rs_xy_scratch(C):
    return [VM((2, 2, 4, 32, C), bf16), VM((2, 2, 2, 4, 32, C), bf16),
            VM((2, 2, 32, C), bf16), VM((2, 2, 2, 32, C), bf16), VM((2, 4, 64, C), bf16)]


def rs_xy_gens(w, me, g, out, t1, r1, t2, r2, mid):
    x, y = me.x, me.y

    def half(k, first, second):
        base = k * 64
        if first == "y":
            pick = lambda i, o: g.at[:, i, pl.ds(base + o, 32)]
        else:
            pick = lambda i, o: g.at[i, :, pl.ds(base + o, 32)]
        yield from ring_scatter(w, me, first, lambda i: pick(i, 0), lambda i: pick(i, 32), t1.at[k, 0], t1.at[k, 1],
                                (r1.at[k, 0, 0], r1.at[k, 0, 1]), (r1.at[k, 1, 0], r1.at[k, 1, 1]), loop_add)
        p = me.pos(first)
        m = mid.at[k]
        for hh in range(2):
            own = pick(p, 32 * hh)

            def body(i, _):
                def inner(j, _):
                    s = pl.ds(pl.multiple_of(j * 16, 16), 16)
                    d = pl.ds(pl.multiple_of(j * 16 + 32 * hh, 16), 16)
                    v = own[i, s].astype(f32) + r1[k, 0, hh, i, s].astype(f32) + r1[k, 1, hh, i, s].astype(f32)
                    m[i, d] = v.astype(bf16)
                    return 0
                return lax.fori_loop(0, 2, inner, 0)
            lax.fori_loop(0, 4, body, 0)
        yield
        q = me.pos(second)
        add1 = lambda dst, a: loop_add(dst, a)
        pick2 = lambda i, o: mid.at[k, i, pl.ds(o, 32)]

        def add2(dst, a):
            def inner(j, _):
                s = pl.ds(pl.multiple_of(j * 16, 16), 16)
                dst[s] = (dst[s].astype(f32) + a[s].astype(f32)).astype(bf16)
                return 0
            lax.fori_loop(0, 2, inner, 0)
        yield from ring_scatter(w, me, second, lambda i: pick2(i, 0), lambda i: pick2(i, 32), t2.at[k, 0], t2.at[k, 1],
                                (r2.at[k, 0, 0], r2.at[k, 0, 1]), (r2.at[k, 1, 0], r2.at[k, 1, 1]), add2)
        for hh in range(2):
            def inner(j, _):
                s = pl.ds(pl.multiple_of(j * 16, 16), 16)
                d = pl.ds(pl.multiple_of(j * 16 + 32 * hh, 16), 16)
                dd = pl.ds(pl.multiple_of(j * 16 + 32 * hh + base, 16), 16)
                v = m[q, d].astype(f32) + r2[k, 0, hh, s].astype(f32) + r2[k, 1, hh, s].astype(f32)
                out[dd] = v.astype(out.dtype)
                return 0
            lax.fori_loop(0, 2, inner, 0)
    return [half(0, "y", "x"), half(1, "x", "y")]


def rs_xy(g, cid, out_dtype=f32):
    C = g.shape[-1]

    def kernel(gin, out, send, recv, *scr):
        me = Place()
        meet([me.step("x", 1), me.step("x", -1), me.step("y", 1), me.step("y", -1)])
        w = Wire(send, recv)
        run(rs_xy_gens(w, me, gin, out, *scr))
        w.finish()

    return pl.pallas_call(
        kernel, out_shape=jax.ShapeDtypeStruct((128, C), out_dtype),
        in_specs=[pl.BlockSpec(memory_space=VM)], out_specs=pl.BlockSpec(memory_space=VM),
        scratch_shapes=[pltpu.SemaphoreType.DMA((24,)), pltpu.SemaphoreType.DMA((24,))] + rs_xy_scratch(C),
        compiler_params=params(cid, 60))(g)


def ag_z_gen(w, me, src, out):
    sib = me.sibling()
    blk = lambda i, cc: out.at[lax.div(i, 2), cc, lax.rem(i, 2)]
    cs = []

    def to_sib(ref):
        cs.append(w.go(ref, ref, sib))
    whole = lambda i: blk(i, me.c)
    own = w.go(src, whole(me.z), sib)
    yield from ring_gather(w, me, "z", whole, lambda i: whole(i).at[pl.ds(0, 64)], lambda i: whole(i).at[pl.ds(64, 64)],
                           first=src, arrived=to_sib)
    own.wait_recv()
    for c in cs:
        c.wait_recv()


def ag_z(shard, cid, space=VM):
    C = shard.shape[1]

    def kernel(src, out, send, recv, lsem):
        me = Place()
        meet([me.step("z", 1), me.step("z", -1), me.sibling()])
        w = Wire(send, recv)
        lc = pltpu.make_async_copy(src, out.at[me.h, me.c, me.l], lsem)
        lc.start()
        lc.wait()
        run([ag_z_gen(w, me, src, out)])
        w.finish()

    return pl.pallas_call(
        kernel, out_shape=jax.ShapeDtypeStruct((2, 2, 2, 128, C), shard.dtype),
        in_specs=[pl.BlockSpec(memory_space=space)], out_specs=pl.BlockSpec(memory_space=space),
        scratch_shapes=[pltpu.SemaphoreType.DMA((16,)), pltpu.SemaphoreType.DMA((16,)), pltpu.SemaphoreType.DMA],
        compiler_params=params(cid))(shard)


def rs_z_scratch(C):
    return [VM((4, 128, C), bf16), VM((2, 64, C), bf16), VM((2, 2, 64, C), bf16)]


def rs_z_gen(w, me, g, out, sibs, t, r):
    sib = me.sibling()
    oc = 1 - me.c
    order = [2, 1, 3, 0]
    blk = lambda i, cc: g.at[lax.div(i, 2), cc, lax.rem(i, 2)]
    z = me.z
    sc = {}
    for o in order:
        i = m4(z + o)
        sc[o] = w.go(blk(i, oc), sibs.at[i], sib)
    yield

    def fold(o, s0, n):
        i = m4(z + o)
        b = blk(i, me.c)

        def inner(j, _):
            s = pl.ds(pl.multiple_of(j * 16 + s0, 16), 16)
            sibs[i, s] = (sibs[i, s].astype(f32) + b[s].astype(f32)).astype(bf16)
            return 0
        lax.fori_loop(0, n // 16, inner, 0)
    up, down = me.step("z", 1), me.step("z", -1)
    half = lambda o, k: sibs.at[m4(z + o), pl.ds(64 * k, 64)]
    sc[2].wait_recv()
    fold(2, 0, 64)
    ta = w.go(half(2, 0), t.at[0], up)
    fold(2, 64, 64)
    tb = w.go(half(2, 1), t.at[1], down)
    sc[1].wait_recv()
    fold(1, 64, 64)
    da = w.go(half(1, 1), r.at[0, 1], up)
    sc[3].wait_recv()
    fold(3, 0, 64)
    db = w.go(half(3, 0), r.at[1, 0], down)
    fold(1, 0, 64)
    fold(3, 64, 64)
    yield

    def add(dst, a):
        def inner(j, _):
            s = pl.ds(pl.multiple_of(j * 16, 16), 16)
            dst[s] = (dst[s].astype(f32) + a[s].astype(f32)).astype(bf16)
            return 0
        lax.fori_loop(0, 4, inner, 0)
    ta.wait_recv()
    add(t.at[0], half(1, 0))
    sa = w.go(t.at[0], r.at[0, 0], up)
    tb.wait_recv()
    add(t.at[1], half(3, 1))
    sb = w.go(t.at[1], r.at[1, 1], down)
    sc[0].wait_recv()
    own = blk(z, me.c)
    yield

    def last(hh):
        def inner(j, _):
            s = pl.ds(pl.multiple_of(j * 16, 16), 16)
            d = pl.ds(pl.multiple_of(j * 16 + 64 * hh, 16), 16)
            v = own[d].astype(f32) + sibs[z, d].astype(f32) + r[0, hh, s].astype(f32) + r[1, hh, s].astype(f32)
            out[d] = v.astype(out.dtype)
            return 0
        lax.fori_loop(0, 4, inner, 0)
    da.wait_recv()
    sa.wait_recv()
    db.wait_recv()
    sb.wait_recv()
    last(0)
    last(1)


def rs_z(g, cid, out_dtype=f32):
    C = g.shape[-1]

    def kernel(gin, out, send, recv, *scr):
        me = Place()
        meet([me.step("z", 1), me.step("z", -1), me.sibling()])
        w = Wire(send, recv)
        run([rs_z_gen(w, me, gin, out, *scr)])
        w.finish()

    return pl.pallas_call(
        kernel, out_shape=jax.ShapeDtypeStruct((128, C), out_dtype),
        in_specs=[pl.BlockSpec(memory_space=VM)], out_specs=pl.BlockSpec(memory_space=VM),
        scratch_shapes=[pltpu.SemaphoreType.DMA((16,)), pltpu.SemaphoreType.DMA((16,))] + rs_z_scratch(C),
        compiler_params=params(cid))(g)


def swap_devs(me):
    out = []
    for dh, dc in ((0, 1), (1, 0), (1, 1)):
        h = lax.rem(me.h + dh, 2)
        c = lax.rem(me.c + dc, 2)
        out.append((h * 2 + c, me.at(z=h * 2 + me.l, c=c)))
    return out


def swap_hc(parts, cid):
    n = len(parts)

    def kernel(*refs):
        ins, outs = refs[:n], refs[n:2 * n]
        send, recv, lsem = refs[2 * n:]
        me = Place()
        peers = swap_devs(me)
        meet([d for _, d in peers])
        w = Wire(send, recv)
        mine = me.h * 2 + me.c
        arrivals = []
        for j, d in reversed(peers):
            for a, b in zip(ins, outs):
                arrivals.append(w.go(a.at[j], b.at[mine], d))
        ls = []
        for k, (a, b) in enumerate(zip(ins, outs)):
            lc = pltpu.make_async_copy(a.at[mine], b.at[mine], lsem.at[k])
            lc.start()
            ls.append(lc)
        for lc in ls:
            lc.wait()
        for a in arrivals:
            a.wait_recv()
        w.finish()

    return pl.pallas_call(
        kernel, out_shape=[jax.ShapeDtypeStruct(p.shape, p.dtype) for p in parts],
        in_specs=[pl.BlockSpec(memory_space=VM)] * n, out_specs=[pl.BlockSpec(memory_space=VM)] * n,
        scratch_shapes=[pltpu.SemaphoreType.DMA((3 * n,)), pltpu.SemaphoreType.DMA((3 * n,)),
                        pltpu.SemaphoreType.DMA((n,))],
        compiler_params=params(cid))(*parts)


def sum_all(v, cid):
    R, C = v.shape

    def kernel(src, out, z_in, x_in, y_in, acc, send, recv):
        me = Place()
        zs = []
        for dz in range(4):
            for dc in range(2):
                if dz or dc:
                    z, c = m4(me.z + dz), lax.rem(me.c + dc, 2)
                    zs.append(me.at(z=z, c=c))
        xs = [me.step("x", d) for d in (1, 2, 3)]
        ys = [me.step("y", d) for d in (1, 2, 3)]
        meet(zs + xs + ys)
        w = Wire(send, recv)
        acc[...] = src[...]
        for buf, slot, devs, n in ((z_in, me.z * 2 + me.c, zs, 8), (x_in, me.x, xs, 4), (y_in, me.y, ys, 4)):
            buf[slot] = acc[...]
            cs = [w.go(buf.at[slot], buf.at[slot], d) for d in devs]
            for c in cs:
                c.wait_recv()
            total = buf[0]
            for k in range(1, n):
                total = total + buf[k]
            w.finish()
            acc[...] = total
        out[...] = acc[...]

    return pl.pallas_call(
        kernel, out_shape=jax.ShapeDtypeStruct((R, C), f32),
        in_specs=[pl.BlockSpec(memory_space=VM)], out_specs=pl.BlockSpec(memory_space=VM),
        scratch_shapes=[VM((8, R, C), f32), VM((4, R, C), f32), VM((4, R, C), f32), VM((R, C), f32),
                        pltpu.SemaphoreType.DMA((13,)), pltpu.SemaphoreType.DMA((13,))],
        compiler_params=params(cid))(v)


from jax.sharding import PartitionSpec as P

D = 2048
HD = 64
STEP = 10
SEQ = 256
PACKS = 4
ROWS = 1024
epsilon = 1e-06
rope_base = 1000000.0
beta_one = 0.9
beta_two = 0.999
adam_epsilon = 1e-08
weight_decay = 0.1
gain_rate = 0.3
masked_score = -1000000000.0
PLANE = [[x * 16 + y * 4 + k for x in range(4) for y in range(4)] for k in range(4)]


def rows_product(left, right):
    return lax.dot_general(left, right, (((0,), (0,)), ((), ())), preferred_element_type=f32)


def column_product(left, right):
    return lax.dot_general(left, right, (((1,), (1,)), ((), ())), preferred_element_type=f32)


def product(left, right):
    return jnp.dot(left, right, preferred_element_type=f32)


def norm_forward(values, gain):
    inverse = lax.rsqrt(jnp.mean(values * values, axis=-1, keepdims=True) + epsilon)
    return (values * inverse * gain, inverse)


def norm_backward(values, inverse, gain, upstream):
    scaled = upstream * gain
    inner = jnp.mean(values * scaled, axis=-1, keepdims=True)
    return (inverse * (scaled - values * inverse * inverse * inner), upstream * values * inverse)


def positions_of(rows):
    places = jnp.arange(SEQ, dtype=jnp.int32)[None, :]
    fresh = jnp.concatenate([jnp.ones((rows.shape[0], 1), jnp.bool_), rows[:, 1:] != rows[:, :-1]], axis=1)
    starts = jnp.where(fresh, places, 0)
    return places - lax.cummax(starts, axis=1)


def rope_tables(positions):
    half_dim = HD // 2
    frequency = rope_base ** (-2.0 * jnp.arange(half_dim, dtype=f32) / HD)
    angles = positions.astype(f32)[..., None] * frequency
    return (jnp.cos(angles), jnp.sin(angles))


def rotate(values, cosine, sine):
    front, back = values[..., : HD // 2], values[..., HD // 2 :]
    return jnp.concatenate([front * cosine - back * sine, back * cosine + front * sine], axis=-1)


def adam_step(weights_now, moment_now, square_now, gradient, step_rate, decay_rate):
    momentum = beta_one * moment_now + (1.0 - beta_one) * gradient
    variance = beta_two * square_now + (1.0 - beta_two) * gradient * gradient
    ratio = momentum / (1.0 - beta_one**STEP) / (jnp.sqrt(variance / (1.0 - beta_two**STEP)) + adam_epsilon)
    return (weights_now - step_rate * (ratio + decay_rate * weights_now), momentum, variance)


def split_out(parts):
    return jnp.concatenate([p.reshape(32, 4, -1) for p in parts], axis=2).transpose(1, 0, 2)


def join_back(whole, widths):
    out, at = [], 0
    for n in widths:
        out.append(whole[:, :, at : at + n].transpose(1, 0, 2).reshape(32, 4 * n))
        at += n
    return out


def gather_plane(shard):
    return lax.all_gather(shard, "dp", axis_index_groups=PLANE, axis=0, tiled=True)


def scatter_plane(whole):
    return lax.psum_scatter(whole, "dp", axis_index_groups=PLANE, scatter_dimension=0, tiled=True)


def gather_tokens(shard):
    return ag_z(shard, 3).reshape(ROWS, D)


def scatter_tokens(whole):
    return rs_z(whole.astype(bf16).reshape(2, 2, 2, 128, D), 4)


def local(
    block_input, output_grad, segment_ids, norm_gains, gain_moment, gain_square,
    query_weight, query_moment, query_square, key_weight, key_moment, key_square,
    value_weight, value_moment, value_square, output_weight, output_moment, output_square,
    gate_weight, gate_moment, gate_square, up_weight, up_moment, up_square,
    down_weight, down_moment, down_square,
):
    gain_one = norm_gains[:D]
    gain_two = norm_gains[D : 2 * D]
    gain_query = norm_gains[2 * D : 2 * D + HD]
    gain_key = norm_gains[2 * D + HD :]
    low = lambda w: w.astype(bf16)
    front_out = split_out([low(query_weight), low(key_weight), low(value_weight), low(output_weight)])
    rest_out = split_out([low(gate_weight), low(up_weight), low(down_weight)])
    segment_out = jnp.broadcast_to(segment_ids[None], (4, 8, SEQ))
    front_shard, rest_shard, segments = swap_hc([front_out, rest_out, segment_out], 1)
    front_full = gather_plane(front_shard.reshape(128, 640))
    rest_full = gather_plane(rest_shard.reshape(128, 3072))
    qkv_full, output_full = front_full[:, :384], front_full[:, 384:]
    gate_up_full, down_full = rest_full[:, :2048], rest_full[:, 2048:]

    rows_in = block_input.astype(f32)
    normed_one, inverse_one = norm_forward(rows_in, gain_one)
    gathered_one = gather_tokens(normed_one.astype(bf16))
    gathered_cot = gather_tokens(output_grad)

    packs = segments[:, 0, :]
    cosine, sine = rope_tables(positions_of(packs))
    places = jnp.arange(SEQ, dtype=jnp.int32)
    allowed = (packs[:, :, None] == packs[:, None, :]) & (places[None, None, :] <= places[None, :, None])
    score_scale = HD ** (-0.5)

    qkv = product(gathered_one, qkv_full)
    query_pre = qkv[:, :256].reshape(PACKS, SEQ, 4, HD)
    key_pre = qkv[:, 256:320].reshape(PACKS, SEQ, HD)
    value_low = qkv[:, 320:].astype(bf16).reshape(PACKS, SEQ, HD)
    query_normed, query_inverse = norm_forward(query_pre, gain_query)
    key_normed, key_inverse = norm_forward(key_pre, gain_key)
    query_rot = rotate(query_normed, cosine[:, :, None, :], sine[:, :, None, :]).astype(bf16)
    key_rot = rotate(key_normed, cosine, sine).astype(bf16)
    scores = jnp.einsum("pqjd,pkd->pjqk", query_rot, key_rot, preferred_element_type=f32) * score_scale
    scores = jnp.where(allowed[:, None], scores, masked_score)
    exps = jnp.exp(scores - jnp.max(scores, axis=-1, keepdims=True))
    probs = exps / jnp.sum(exps, axis=-1, keepdims=True)
    probs_low = probs.astype(bf16)
    mixed = jnp.einsum("pjqk,pkd->pqjd", probs_low, value_low, preferred_element_type=f32)
    mixed_low = mixed.astype(bf16).reshape(ROWS, 256)

    middle = rows_in + scatter_tokens(column_product(mixed_low, output_full))
    normed_two, inverse_two = norm_forward(middle, gain_two)
    gathered_two = gather_tokens(normed_two.astype(bf16))
    gate_up = product(gathered_two, gate_up_full)
    gate_pre, up_pre = gate_up[:, :1024], gate_up[:, 1024:]
    sigmoid_gate = jax.nn.sigmoid(gate_pre)
    silu_gate = gate_pre * sigmoid_gate
    hidden_low = (silu_gate * up_pre).astype(bf16)

    hidden_grad = product(gathered_cot, down_full)
    up_low = (hidden_grad * silu_gate).astype(bf16)
    gate_low = (hidden_grad * up_pre * (sigmoid_gate + silu_gate * (1.0 - sigmoid_gate))).astype(bf16)
    gate_up_low = jnp.concatenate([gate_low, up_low], axis=1)
    gate_up_grad = rows_product(gathered_two, gate_up_low)
    down_grad = rows_product(gathered_cot, hidden_low)
    rest_grad = jnp.concatenate([gate_up_grad.astype(bf16), down_grad.astype(bf16)], axis=1)
    rest_mine = scatter_plane(rest_grad)

    normed_two_grad = scatter_tokens(column_product(gate_up_low, gate_up_full))
    block_output = middle + scatter_tokens(column_product(hidden_low, down_full))
    middle_back, gain_two_terms = norm_backward(middle, inverse_two, gain_two, normed_two_grad)
    middle_grad = output_grad.astype(f32) + middle_back
    gathered_attn = gather_tokens(middle_grad.astype(bf16))
    mixed_grad = product(gathered_attn, output_full).astype(bf16).reshape(PACKS, SEQ, 4, HD)
    output_weight_grad = rows_product(gathered_attn, mixed_low)

    prob_grad = jnp.einsum("pqjd,pkd->pjqk", mixed_grad, value_low, preferred_element_type=f32)
    inner_term = jnp.sum(probs * prob_grad, axis=-1, keepdims=True)
    score_grad = (probs * (prob_grad - inner_term)).astype(bf16)
    query_rot_grad = jnp.einsum("pjqk,pkd->pqjd", score_grad, key_rot, preferred_element_type=f32) * score_scale
    key_rot_grad = jnp.einsum("pjqk,pqjd->pkd", score_grad, query_rot, preferred_element_type=f32) * score_scale
    value_grad = jnp.einsum("pjqk,pqjd->pkd", probs_low, mixed_grad, preferred_element_type=f32).astype(bf16)
    query_pre_grad, gain_query_terms = norm_backward(
        query_pre, query_inverse, gain_query, rotate(query_rot_grad, cosine[:, :, None, :], -sine[:, :, None, :])
    )
    key_pre_grad, gain_key_terms = norm_backward(key_pre, key_inverse, gain_key, rotate(key_rot_grad, cosine, -sine))
    qkv_low = jnp.concatenate(
        [query_pre_grad.astype(bf16).reshape(ROWS, 256), key_pre_grad.astype(bf16).reshape(ROWS, HD),
         value_grad.reshape(ROWS, HD)], axis=1
    )
    qkv_grad = rows_product(gathered_one, qkv_low)
    front_grad = jnp.concatenate([qkv_grad.astype(bf16), output_weight_grad.astype(bf16)], axis=1)
    front_mine = scatter_plane(front_grad)
    normed_one_grad = scatter_tokens(column_product(qkv_low, qkv_full))
    input_back, gain_one_terms = norm_backward(rows_in, inverse_one, gain_one, normed_one_grad)
    input_grad = middle_grad + input_back

    gain_local = jnp.concatenate(
        [jnp.sum(gain_one_terms, axis=0), jnp.sum(gain_two_terms, axis=0),
         jnp.sum(gain_query_terms, axis=(0, 1, 2)), jnp.sum(gain_key_terms, axis=(0, 1))]
    )
    gain_grads = sum_all(gain_local.reshape(33, 128), 5).reshape(-1)

    front_back, rest_back = swap_hc([front_mine.reshape(4, 32, 640), rest_mine.reshape(4, 32, 3072)], 2)
    sums = join_back(front_back.astype(f32), (256, 64, 64, 256)) + join_back(rest_back.astype(f32), (1024, 1024, 1024))
    results = [block_output, input_grad]
    results += adam_step(norm_gains, gain_moment, gain_square, gain_grads, gain_rate, 0.0)
    states = (
        (query_weight, query_moment, query_square, 0.04), (key_weight, key_moment, key_square, 0.04),
        (value_weight, value_moment, value_square, 0.04), (output_weight, output_moment, output_square, 0.15),
        (gate_weight, gate_moment, gate_square, 0.04), (up_weight, up_moment, up_square, 0.04),
        (down_weight, down_moment, down_square, 0.02),
    )
    for (w, m, v, rate), grad in zip(states, sums):
        results += adam_step(w, m, v, grad, rate, weight_decay)
    return tuple(results)


def solution(mesh):
    tokens, weight = P(("dp", "tensor"), None), P("dp", "tensor")
    in_specs = (tokens, tokens, P("dp", None), P(), P(), P()) + (weight,) * 21
    out_specs = (tokens, tokens, P(), P(), P()) + (weight,) * 21
    return jax.shard_map(local, mesh=mesh, in_specs=in_specs, out_specs=out_specs, check_vma=False)
```

time: 3450 us -> 533 us (0.15)
  waiting for transfers between devices: 3120 us -> 28.2 us
  Pallas kernels: 0 us -> 279 us
  blocking collectives: 67.2 us -> 0 us
  matrix products: 163 us -> 101 us
    reduce_scatter x11 -> x2, waiting for transfers between devices: 2460 us -> 27.5 us  [scatter_plane(): lax.psum_scatter(whole, 'dp', axis_index_groups=PLANE, scatter_dimension=...]
    all_gather x11 -> x2, waiting for transfers between devices: 653 us -> 0.02 us  [gather_plane(): lax.all_gather(shard, 'dp', axis_index_groups=PLANE, axis=0, tiled=True)]
    pallas_call x0 -> x11, Pallas kernels: none -> 279 us  [the longest x4 120 us: ag_z(): pl.pallas_call(kernel, out_shape=jax.ShapeDtypeStruct((2, 2, 2, 128, C),...]
    psum x1 -> x0, blocking collectives: 67.2 us -> none  [local(): gain_grads = lax.psum(gain_local, ('dp', 'tensor'))]
  transfers between devices with their start and end apart: 22 -> 4, of which waited for: 20 -> 1; matrix products, arithmetic and copies ran while one was open for 4% -> 21% of each run, Pallas kernels for 0% -> 34%
where the time goes in v1:
time: 533 us; the launch traced here: 523 us
  Pallas kernels  279 us (52%)
  matrix products  101 us (19%)
  other arithmetic  58.1 us (11%)
  local copies, waits for them, and re-layouts  40.5 us (8%)
  waiting for transfers between devices  28.2 us (5%)
  between operations  15.4 us (3%)
    pallas_call x4, Pallas kernels, ag_z(): pl.pallas_call(kernel, out_shape=jax.ShapeDtypeStruct((2, 2, 2, 128, C),...  120 us
    pallas_call x4, Pallas kernels, rs_z(): pl.pallas_call(kernel, out_shape=jax.ShapeDtypeStruct((128, C), out_dtype...  106 us
    pallas_call x2, Pallas kernels, swap_hc(): pl.pallas_call(kernel, out_shape=[jax.ShapeDtypeStruct(p.shape, p.dtype)...  36.1 us
    dot_general x4, matrix products, column_product(): lax.dot_general(left, right, (((1,), (1,)), ((), ())), preferred_element_...  32.7 us
    dot_general x4, matrix products, product(): return jnp.dot(left, right, preferred_element_type=f32)  30 us
    reduce_scatter x2, waiting for transfers between devices, scatter_plane(): lax.psum_scatter(whole, 'dp', axis_index_groups=PLANE, scatter_dimension=...  27.5 us
    unnamed x146, local copies, waits for them, and re-layouts  26.6 us
    dot_general x4, matrix products, rows_product(): lax.dot_general(left, right, (((0,), (0,)), ((), ())), preferred_element_...  26.2 us
  transfers between devices with their start and end apart: 4, of which 1 were waited for; matrix products, arithmetic and copies ran while one was open for 21% of the time, Pallas kernels for 34%

profile of v1, /device:TPU:1, one launch (start us, length us, event | category | flops | bytes accessed | tf_op | source)
XLA Modules:
  0.0 523.2 jit_solution(10761428126749142845)
XLA Ops:
  9.0 0.9 convert_element_type.116
  9.9 1.0 convert_element_type.119
  10.9 1.1 convert_element_type.120
  12.0 1.1 convert_element_type.121
  13.1 1.1 convert_element_type.122
  14.2 0.9 maximum_bitcast_fusion.refs_1_
  16.5 19.0 %shard_map.459 = (bf16[4,32,640]{2,1,0:T(8,128)(2,1)}, bf16[4,32,3072]{2,1,0:T(8,128)(2,1)}, s32[4,8,256]{2,1,0:T(8,128)}) custom-call(bf16[4,32,640]{2,1,0:T(8,128)(2,1)} %maximum_bitcast_fusion.1.refs_0_, bf16[4,32,3072]{2,1,0:T(8,128)(2,1)} %maximum_bitcast_fusion.refs_1_, s32[4,8,256]{2,1,0:T(8,128)} %broadcast_in_dim.23.refs_2_), custom_call_target="tpu_custom_call" | custom-call | tf_op jit(solution)/shard_map/pallas_call | solution.py:421
  38.1 1.2 reduce-window.6
  39.8 1.0 fusion.31.src
  40.8 27.4 %shard_map.458 = bf16[2,2,2,128,2048]{4,3,2,1,0:T(8,128)(2,1)} custom-call(bf16[128,2048]{1,0:T(8,128)(2,1)} %fusion.31.src), custom_call_target="tpu_custom_call" | custom-call | tf_op jit(solution)/shard_map/pallas_call | solution.py:288
  68.2 28.0 %shard_map.463 = bf16[2,2,2,128,2048]{4,3,2,1,0:T(8,128)(2,1)} custom-call(bf16[128,2048]{1,0:T(8,128)(2,1)} %src.1), custom_call_target="tpu_custom_call" | custom-call | tf_op jit(solution)/shard_map/pallas_call | solution.py:288
  96.9 1.0 compare_and_fusion
  97.9 4.5 fusion.22
  102.4 1.1 slice.141
  104.4 1.7 reshape.316
  106.5 1.2 copy.267
  107.7 1.2 fusion.59
  109.0 0.9 multiply_multiply_fusion.1
  109.8 0.9 subtract_convert_fusion
  110.7 4.7 fusion.104
  115.4 2.7 fusion.27
  118.6 4.8 convolution_convert_fusion.2
  123.4 26.4 %shard_map.460 = f32[128,2048]{1,0:T(8,128)} custom-call(bf16[2,2,2,128,2048]{4,3,2,1,0:T(8,128)(2,1)} %bitcast.193), custom_call_target="tpu_custom_call" | custom-call | tf_op jit(solution)/shard_map/pallas_call | solution.py:379
  149.8 1.5 multiply_reduce_fusion.4
  151.3 0.9 multiply_convert_fusion.1.src
  152.2 26.7 %shard_map.461 = bf16[2,2,2,128,2048]{4,3,2,1,0:T(8,128)(2,1)} custom-call(bf16[128,2048]{1,0:T(8,128)(2,1)} %multiply_convert_fusion.1.src), custom_call_target="tpu_custom_call" | custom-call | tf_op jit(solution)/shard_map/pallas_call | solution.py:288
  179.0 12.9 %fusion.3 = f32[1024,2048]{1,0:T(8,128)S(1)} fusion(bf16[1024,2048]{1,0:T(8,128)(2,1)} %bitcast.201, bf16[2048,3072]{1,0:T(8,128)(2,1)} %all-gather.5.cloned.1.call-done), kind=kOutput, calls=%fused_computation.5 | convolution fusion | flops 8589934592 | bytes 20971520 | tf_op jit(solution)/shard_map/dot_general | solution.py:493
  191.9 9.3 %fusion.9 = (bf16[1024,1024]{1,0:T(8,128)(2,1)S(1)}, bf16[1024,1024]{1,0:T(8,128)(2,1)S(1)}, bf16[1024,1024]{1,0:T(8,128)(2,1)}) fusion(f32[1024,2048]{1,0:T(8,128)S(1)} %fusion.3, bf16[1024,2048]{1,0:T(8,128)(2,1)S(1)} %bitcast.198, bf16[2048,3072]{1,0:T(8,128)(2,1)} %all-gather.5.cloned.1.call-done), kind=kOutput, calls=%fused_computation.16 | convolution fusion | flops 4309647360 | bytes 23068672 | tf_op jit(solution)/shard_map/dot_general | solution.py:493
  201.3 1.3 copy-done.67
  202.6 12.7 %fusion.11 = bf16[1024,2048]{1,0:T(8,128)(2,1)} fusion(bf16[2048,3072]{1,0:T(8,128)(2,1)} %all-gather.5.cloned.1.call-done, bf16[1024,1024]{1,0:T(8,128)(2,1)S(1)} %get-tuple-element.69, bf16[1024,1024]{1,0:T(8,128)(2,1)S(1)} %get-tuple-element.68), kind=kOutput, calls=%fused_computation.25 | convolution fusion | flops 8600420352 | bytes 16777216 | tf_op jit(solution)/shard_map/dot_general | solution.py:489
  215.3 26.3 %shard_map.464 = f32[128,2048]{1,0:T(8,128)} custom-call(bf16[2,2,2,128,2048]{4,3,2,1,0:T(8,128)(2,1)} %bitcast.196), custom_call_target="tpu_custom_call" | custom-call | tf_op jit(solution)/shard_map/pallas_call | solution.py:379
  241.6 2.1 multiply_reduce_fusion.1
  243.7 2.4 fusion.92.src
  246.2 37.8 %shard_map.465 = bf16[2,2,2,128,2048]{4,3,2,1,0:T(8,128)(2,1)} custom-call(bf16[128,2048]{1,0:T(8,128)(2,1)} %fusion.92.src), custom_call_target="tpu_custom_call" | custom-call | tf_op jit(solution)/shard_map/pallas_call | solution.py:288
  284.0 4.6 convolution_convert_fusion.5
  288.6 3.3 convolution_convert_fusion.6
  291.9 2.8 reshape.348
  294.6 2.2 copy.209
  296.8 3.2 fusion.30
  301.4 0.9 fusion.7
  307.1 1.3 copy-done.6
  308.5 1.8 convolution_convert_fusion.4
  310.3 1.8 pad_maximum_fusion.4
  312.1 4.4 copy.243
  316.6 7.5 %convert_bitcast_fusion = bf16[2048,1024]{0,1:T(8,128)(2,1)S(1)} fusion(bf16[1024,1024]{1,0:T(8,128)(2,1)} %get-tuple-element.70, bf16[1024,2048]{1,0:T(8,128)(2,1)} %bitcast.197), kind=kOutput, calls=%fused_computation.19 | convolution fusion | flops 4297064448 | bytes 10485760 | tf_op jit(solution)/shard_map/dot_general | solution.py:485
  324.2 12.2 %convolution_convert_fusion = bf16[2048,2048]{0,1:T(8,128)(2,1)S(1)} fusion(bf16[1024,2048]{1,0:T(8,128)(2,1)S(1)} %bitcast.202, bf16[1024,1024]{1,0:T(8,128)(2,1)} %copy-done.67, bf16[1024,1024]{1,0:T(8,128)(2,1)} %copy-done.66), kind=kOutput, calls=%fused_computation.2 | convolution fusion | flops 8602517504 | bytes 16777216 | tf_op jit(solution)/shard_map/dot_general | solution.py:485
  336.4 14.9 %pad_maximum_fusion = bf16[2048,3072]{0,1:T(8,128)(2,1)} fusion(bf16[2048,1024]{0,1:T(8,128)(2,1)S(1)} %convert_bitcast_fusion, bf16[2048,2048]{0,1:T(8,128)(2,1)S(1)} %convolution_convert_fusion), kind=kLoop, calls=%fused_computation.1 | loop fusion | flops 25165824 | bytes 25165824 | tf_op jit(solution)/shard_map/concatenate | solution.py:624
  351.3 16.7 %copy.245 = bf16[2048,3072]{1,0:T(8,128)(2,1)} copy(bf16[2048,3072]{0,1:T(8,128)(2,1)} %pad_maximum_fusion) | data formatting | bytes 25165824
  368.1 9.5 %convolution_convert_fusion.3 = bf16[1024,2048]{1,0:T(8,128)(2,1)} fusion(bf16[1024,1024]{1,0:T(8,128)(2,1)} %get-tuple-element.70, bf16[2048,3072]{1,0:T(8,128)(2,1)} %all-gather.5.cloned.1.call-done), kind=kOutput, calls=%fused_computation.27 | convolution fusion | flops 4297064448 | bytes 10485760 | tf_op jit(solution)/shard_map/dot_general | solution.py:489
  377.5 26.3 %shard_map.462 = f32[128,2048]{1,0:T(8,128)} custom-call(bf16[2,2,2,128,2048]{4,3,2,1,0:T(8,128)(2,1)} %bitcast.195), custom_call_target="tpu_custom_call" | custom-call | tf_op jit(solution)/shard_map/pallas_call | solution.py:379
  403.9 5.8 %convolution_convert_fusion.1 = bf16[1024,2048]{1,0:T(8,128)(2,1)} fusion(bf16[2048,640]{1,0:T(8,128)(2,1)} %all-gather.3.cloned.1.call-done, bf16[1024,64]{0,1:T(8,128)(2,1)S(1)} %bitcast.233, bf16[1024,64]{0,1:T(8,128)(2,1)S(1)} %multiply_convert_fusion.2, bf16[1024,256]{0,1:T(8,128)(2,1)S(1)} %copy-done.24), kind=kOutput, calls=%fused_computation.24 | convolution fusion | flops 1615069184 | bytes 6553600 | tf_op jit(solution)/shard_map/dot_general | solution.py:489
  409.8 27.4 %shard_map.466 = f32[128,2048]{1,0:T(8,128)} custom-call(bf16[2,2,2,128,2048]{4,3,2,1,0:T(8,128)(2,1)} %bitcast.194), custom_call_target="tpu_custom_call" | custom-call | tf_op jit(solution)/shard_map/pallas_call | solution.py:379
  437.1 1.5 fusion.43
  439.4 17.0 %shard_map.467 = f32[33,128]{1,0:T(8,128)} custom-call(f32[33,128]{1,0:T(8,128)} %bitcast.238), custom_call_target="tpu_custom_call" | custom-call | tf_op jit(solution)/shard_map/pallas_call | solution.py:457
  456.4 1.4 multiply_subtract_fusion.8
  457.8 3.5 fusion.35
  461.2 27.5 %reduce-scatter.9.cloned.1.call-done = bf16[128,3072]{1,0:T(8,128)(2,1)} async-done(((bf16[2048,3072]{1,0:T(8,128)(2,1)}), bf16[128,3072]{1,0:T(8,128)(2,1)}) %reduce-scatter.9.cloned.1.call-update) | async-done | bytes 786448 | tf_op jit(solution)/shard_map/reduce_scatter | solution.py:550
  488.7 17.1 %shard_map.468 = (bf16[4,32,640]{2,1,0:T(8,128)(2,1)}, bf16[4,32,3072]{2,1,0:T(8,128)(2,1)}) custom-call(bf16[4,32,640]{2,1,0:T(8,128)(2,1)} %bitcast.231, bf16[4,32,3072]{2,1,0:T(8,128)(2,1)} %bitcast.223), custom_call_target="tpu_custom_call" | custom-call | tf_op jit(solution)/shard_map/pallas_call | solution.py:421
  505.8 0.9 convert_element_type.147
  507.3 1.4 convert_element_type.148
  511.3 0.8 multiply_subtract_fusion.4
  512.1 1.4 multiply_subtract_fusion.2
  513.5 1.4 multiply_subtract_fusion.1
  514.9 1.4 multiply_subtract_fusion
  (229 shorter events, 18.4 us)
Async XLA Ops:
  7.2 8.7 %copy-start.65 = (s32[1,256]{1,0:T(1,128)S(1)}, s32[1,256]{1,0:T(1,128)}, u32[]{:S(2)}) copy-start(s32[1,256]{1,0:T(1,128)} %param.29) | copy-start | bytes 3076
  7.2 90.7 %all-gather.3.cloned.1.call-start = ((), (), s32[]{:S(2)}) async-start(), calls=%async_computation.2 | async-start | bytes 2785280 | tf_op jit(solution)/shard_map/all_gather | solution.py:546
  9.9 26.5 %copy-start.41 = (f32[4224]{0:T(1024)S(1)}, f32[4224]{0:T(1024)}, u32[]{:S(2)}) copy-start(f32[4224]{0:T(1024)} %param.30) | copy-start | bytes 50692
  9.9 29.7 %copy-start.1 = (bf16[128,2048]{1,0:T(8,128)(2,1)S(1)}, bf16[128,2048]{1,0:T(8,128)(2,1)}, u32[]{:S(2)}) copy-start(bf16[128,2048]{1,0:T(8,128)(2,1)} %param.27) | copy-start | bytes 1572868
  35.6 143.4 %all-gather.5.cloned.1.call-start = ((), (), s32[]{:S(2)}) async-start(), calls=%async_computation.3 | async-start | bytes 13369344 | tf_op jit(solution)/shard_map/all_gather | solution.py:546
  36.3 424.9 %reduce-scatter.7.cloned.1.call-start = ((), (), s32[]{:S(2)}) async-start(), calls=%async_computation.4 | async-start | bytes 2785280 | tf_op jit(solution)/shard_map/reduce_scatter | solution.py:550
  36.5 71.2 %copy-start.52 = (f32[64]{0:T(128)}, f32[64]{0:T(128)S(1)}, u32[]{:S(2)}) copy-start(f32[64]{0:T(128)S(1)} %get-tuple-element.96) | copy-start | bytes 772
  39.8 56.5 %copy-start.59 = (f32[128]{0:T(128)}, f32[128]{0:T(128)S(1)}, u32[]{:S(2)}) copy-start(f32[128]{0:T(128)S(1)} %add_rsqrt_fusion.3) | copy-start | bytes 1540
  39.8 56.5 %copy-start.39 = (f32[2048]{0:T(1024)}, f32[2048]{0:T(1024)S(1)}, u32[]{:S(2)}) copy-start(f32[2048]{0:T(1024)S(1)} %get-tuple-element.95) | copy-start | bytes 24580
  102.4 2.0 copy-start.2
  110.7 4.7 copy-start.28
  110.7 4.7 copy-start.37
  115.4 2.7 copy-start.50
  118.6 4.8 copy-start.11
  151.3 40.6 %copy-start.54 = (f32[128]{0:T(128)}, f32[128]{0:T(128)S(1)}, u32[]{:S(2)}) copy-start(f32[128]{0:T(128)S(1)} %add_rsqrt_fusion.2) | copy-start | bytes 1540
  179.0 12.9 %copy-start.5 = (bf16[2,2,2,128,2048]{4,3,2,1,0:T(8,128)(2,1)S(1)}, bf16[2,2,2,128,2048]{4,3,2,1,0:T(8,128)(2,1)}, u32[]{:S(2)}) copy-start(bf16[2,2,2,128,2048]{4,3,2,1,0:T(8,128)(2,1)} %shard_map.463) | copy-start | bytes 12582916
  201.2 14.0 %copy-start.66 = (bf16[1024,1024]{1,0:T(8,128)(2,1)}, bf16[1024,1024]{1,0:T(8,128)(2,1)S(1)}, u32[]{:S(2)}) copy-start(bf16[1024,1024]{1,0:T(8,128)(2,1)S(1)} %get-tuple-element.68) | copy-start | bytes 6291460
  215.3 26.3 %copy-start.55 = (f32[128]{0:T(128)S(1)}, f32[128]{0:T(128)}, u32[]{:S(2)}) copy-start(f32[128]{0:T(128)} %copy-done.54) | copy-start | bytes 1540
  215.3 28.4 %copy-start.4 = (bf16[128,2048]{1,0:T(8,128)(2,1)S(1)}, bf16[128,2048]{1,0:T(8,128)(2,1)}, u32[]{:S(2)}) copy-start(bf16[128,2048]{1,0:T(8,128)(2,1)} %src.1) | copy-start | bytes 1572868
  243.7 40.3 %copy-start.12 = (bf16[32,8,4,256]{3,1,2,0:T(8,128)(2,1)S(1)}, bf16[32,8,4,256]{3,1,2,0:T(8,128)(2,1)}, u32[]{:S(2)}) copy-start(bf16[32,8,4,256]{3,1,2,0:T(8,128)(2,1)} %copy-done.11) | copy-start | bytes 1572868
  243.7 44.9 %copy-start.62 = (f32[128]{0:T(128)}, f32[128]{0:T(128)S(1)}, u32[]{:S(2)}) copy-start(f32[128]{0:T(128)S(1)} %broadcast_multiply_fusion.2) | copy-start | bytes 1540
  284.0 4.6 copy-start.8
  296.8 3.6 copy-start.9
  296.8 3.7 copy-start.25
  296.8 3.8 copy-start.38
  296.8 3.8 copy-start.51
  302.4 2.0 copy-start.58
  304.9 1.6 copy-start.10
  306.0 2.4 copy-start.6
  307.1 3.2 copy-start.23
  308.4 1.9 copy-start.16
  316.5 172.1 %reduce-scatter.9.cloned.1.call-start = ((), (), s32[]{:S(2)}) async-start(), calls=%async_computation.5 | async-start | bytes 13369344 | tf_op jit(solution)/shard_map/reduce_scatter | solution.py:550
  316.6 7.6 %copy-start.7 = (bf16[2,2,2,128,2048]{4,3,2,1,0:T(8,128)(2,1)S(1)}, bf16[2,2,2,128,2048]{4,3,2,1,0:T(8,128)(2,1)}, u32[]{:S(2)}) copy-start(bf16[2,2,2,128,2048]{4,3,2,1,0:T(8,128)(2,1)} %shard_map.461) | copy-start | bytes 12582916
  377.5 26.4 %copy-start.24 = (bf16[1024,256]{0,1:T(8,128)(2,1)S(1)}, bf16[1024,256]{0,1:T(8,128)(2,1)}, u32[]{:S(2)}) copy-start(bf16[1024,256]{0,1:T(8,128)(2,1)} %copy-done.23) | copy-start | bytes 1572868
  409.7 27.5 %copy-start.40 = (f32[2048]{0:T(1024)S(1)}, f32[2048]{0:T(1024)}, u32[]{:S(2)}) copy-start(f32[2048]{0:T(1024)} %copy-done.39) | copy-start | bytes 24580
  409.7 27.5 %copy-start.60 = (f32[128]{0:T(128)S(1)}, f32[128]{0:T(128)}, u32[]{:S(2)}) copy-start(f32[128]{0:T(128)} %copy-done.59) | copy-start | bytes 1540
  409.7 29.0 %copy-start.43 = (f32[2048]{0:T(1024)S(1)}, f32[2048]{0:T(1024)}, u32[]{:S(2)}) copy-start(f32[2048]{0:T(1024)} %get-tuple-element.36) | copy-start | bytes 24580
  409.7 46.7 %copy-start.42 = (f32[4224]{0:T(1024)S(1)}, f32[4224]{0:T(1024)}, u32[]{:S(2)}) copy-start(f32[4224]{0:T(1024)} %param.30) | copy-start | bytes 50692
  409.7 46.7 %copy-start.48 = (f32[4224]{0:T(1024)S(1)}, f32[4224]{0:T(1024)}, u32[]{:S(2)}) copy-start(f32[4224]{0:T(1024)} %param.31) | copy-start | bytes 50692
  409.7 46.7 %copy-start.49 = (f32[4224]{0:T(1024)S(1)}, f32[4224]{0:T(1024)}, u32[]{:S(2)}) copy-start(f32[4224]{0:T(1024)} %param.32) | copy-start | bytes 50692
  409.7 48.0 %copy-start = (f32[128,2048]{1,0:T(8,128)S(1)}, f32[128,2048]{1,0:T(8,128)}, u32[]{:S(2)}) copy-start(f32[128,2048]{1,0:T(8,128)} %shard_map.464) | copy-start | bytes 3145732
  409.7 48.0 %copy-start.56 = (f32[128]{0:T(128)S(1)}, f32[128]{0:T(128)}, u32[]{:S(2)}) copy-start(f32[128]{0:T(128)} %copy-done.54) | copy-start | bytes 1540
  409.7 48.0 %copy-start.63 = (f32[128]{0:T(128)S(1)}, f32[128]{0:T(128)}, u32[]{:S(2)}) copy-start(f32[128]{0:T(128)} %copy-done.62) | copy-start | bytes 1540
  507.2 1.8 copy-start.35
  507.2 1.8 copy-start.44
  507.2 1.8 copy-start.45
  507.3 2.5 copy-start.36
  507.3 2.5 copy-start.46
  507.3 2.5 copy-start.47
  507.3 3.1 copy-start.26
  507.3 3.1 copy-start.31
  507.3 3.1 copy-start.32
  508.7 2.5 copy-start.27
  508.7 2.5 copy-start.33
  508.7 2.5 copy-start.34
  508.7 3.3 copy-start.13
  508.7 3.3 copy-start.17
  508.8 3.3 copy-start.18
  508.9 4.5 copy-start.14
  508.9 4.5 copy-start.19
  508.9 4.5 copy-start.20
  511.2 3.6 copy-start.15
  511.2 3.6 copy-start.21
  511.2 3.6 copy-start.22
  (8 other events, 10.7 us)
Sparse Core Ops, SparseCore 0:
  35.7 47.3 all-gather.2
  85.3 89.5 all-gather.4
  316.7 73.1 reduce-scatter.6
  393.2 95.4 reduce-scatter.8

commit v2 on v1

--- a/solution.py
+++ b/solution.py
@@ -1,5 +1,6 @@
 import jax
 import jax.numpy as jnp
+import numpy as np
 from jax import lax
 from jax.experimental import pallas as pl
 from jax.experimental.pallas import tpu as pltpu
@@ -355,7 +356,7 @@
             s = pl.ds(pl.multiple_of(j * 16, 16), 16)
             d = pl.ds(pl.multiple_of(j * 16 + 64 * hh, 16), 16)
             v = own[d].astype(f32) + sibs[z, d].astype(f32) + r[0, hh, s].astype(f32) + r[1, hh, s].astype(f32)
-            out[d] = v.astype(out.dtype)
+            out(d, v)
             return 0
         lax.fori_loop(0, 4, inner, 0)
     da.wait_recv()
@@ -373,7 +374,10 @@
         me = Place()
         meet([me.step("z", 1), me.step("z", -1), me.sibling()])
         w = Wire(send, recv)
-        run([rs_z_gen(w, me, gin, out, *scr)])
+
+        def put(s, v):
+            out[s] = v.astype(out.dtype)
+        run([rs_z_gen(w, me, gin, put, *scr)])
         w.finish()
 
     return pl.pallas_call(
@@ -462,8 +466,6 @@
         compiler_params=params(cid))(v)
 
 
-from jax.sharding import PartitionSpec as P
-
 D = 2048
 HD = 64
 STEP = 10
@@ -478,68 +480,501 @@
 weight_decay = 0.1
 gain_rate = 0.3
 masked_score = -1000000000.0
+score_scale = HD ** (-0.5)
+exact = lax.Precision.HIGHEST
+
+
+def dot(a, b, ca=1, cb=0, precision=None):
+    return lax.dot_general(a, b, (((ca,), (cb,)), ((), ())), precision=precision, preferred_element_type=f32)
+
+
+def chunks(n, body, rows=16):
+    def one(j, _):
+        body(pl.ds(pl.multiple_of(j * rows, rows), rows))
+        return 0
+    lax.fori_loop(0, n // rows, one, 0)
+
+
+def dma_sems(n):
+    return [pltpu.SemaphoreType.DMA((n,)), pltpu.SemaphoreType.DMA((n,))]
+
+
+def vm_specs(n):
+    return [pl.BlockSpec(memory_space=VM)] * n
+
+
+def any_specs(n):
+    return [pl.BlockSpec(memory_space=pl.ANY)] * n
+
+
+def spread_weights(weights, segments, cid):
+    def kernel(q, k, v, o, g, u, d, seg, front, rest, segs, fbuf, rbuf, sbuf, send, recv):
+        me = Place()
+        peers = swap_devs(me)
+        mine = me.h * 2 + me.c
+        for j in range(4):
+            fbuf[j, :, 0:256] = q[:, 256 * j:256 * j + 256].astype(bf16)
+            fbuf[j, :, 256:384] = jnp.concatenate(
+                [k[:, 64 * j:64 * j + 64], v[:, 64 * j:64 * j + 64]], axis=1).astype(bf16)
+            fbuf[j, :, 384:640] = o[:, 256 * j:256 * j + 256].astype(bf16)
+            for i, w in enumerate((g, u, d)):
+                rbuf[j, :, 1024 * i:1024 * i + 1024] = w[:, 1024 * j:1024 * j + 1024].astype(bf16)
+        sbuf[...] = jnp.broadcast_to(seg[...], (8, SEQ))
+        meet([dev for _, dev in peers])
+        w = Wire(send, recv)
+        arrivals = []
+        for j, dev in reversed(peers):
+            arrivals.append(w.go(rbuf.at[j], rest.at[mine], dev))
+            arrivals.append(w.go(fbuf.at[j], front.at[mine], dev))
+            arrivals.append(w.go(sbuf, segs.at[mine], dev))
+        front[mine] = fbuf[mine]
+        rest[mine] = rbuf[mine]
+        segs[mine] = sbuf[...]
+        for a in arrivals:
+            a.wait_recv()
+        w.finish()
+
+    return pl.pallas_call(
+        kernel,
+        out_shape=[jax.ShapeDtypeStruct((4, 32, 640), bf16), jax.ShapeDtypeStruct((4, 32, 3072), bf16),
+                   jax.ShapeDtypeStruct((4, 8, SEQ), jnp.int32)],
+        in_specs=vm_specs(8), out_specs=vm_specs(3),
+        scratch_shapes=[VM((4, 32, 640), bf16), VM((4, 32, 3072), bf16), VM((8, SEQ), jnp.int32)] + dma_sems(9),
+        compiler_params=params(cid))(*weights, segments)
+
+
+def rope_constants():
+    frequency = np.float32(rope_base) ** (np.float32(-2.0) * np.arange(HD // 2, dtype=np.float32) / np.float32(HD))
+    angles = (np.arange(SEQ, dtype=np.float32)[None, :] * frequency[:, None].astype(np.float32)).astype(np.float64)
+    return np.concatenate([np.cos(angles), np.sin(angles)], axis=0).astype(np.float32)
+
+
+def pack_tables(segs, p, table):
+    row = segs[p].astype(f32)[0:1, :]
+    column = jnp.broadcast_to(row, (128, SEQ)).T[:, 0:1]
+    key_at = lax.broadcasted_iota(jnp.int32, (SEQ, SEQ), 0)
+    query_at = lax.broadcasted_iota(jnp.int32, (SEQ, SEQ), 1)
+    allowed = (column == row) & (key_at <= query_at)
+    start = jnp.sum(jnp.where(column < row, 1.0, 0.0), axis=0, keepdims=True)
+    where = query_at.astype(f32) - start
+    hot = jnp.where(key_at.astype(f32) == where, 1.0, 0.0)
+    both = dot(table[...], hot, precision=exact)
+    return allowed, both[0:32], both[32:64]
+
+
+def head_norm(z, gain):
+    inverse = lax.rsqrt(jnp.mean(z * z, axis=0, keepdims=True) + epsilon)
+    return z * inverse * gain, inverse
+
+
+def head_norm_back(z, inverse, gain, up):
+    scaled = up * gain
+    inner = jnp.mean(z * scaled, axis=0, keepdims=True)
+    return inverse * (scaled - z * inverse * inverse * inner), up * z * inverse
+
+
+def turn(u, cosine, sine):
+    a, b = u[0:32], u[32:64]
+    return jnp.concatenate([a * cosine - b * sine, b * cosine + a * sine], axis=0)
+
+
+def turn_back(u, cosine, sine):
+    a, b = u[0:32], u[32:64]
+    return jnp.concatenate([a * cosine + b * sine, b * cosine - a * sine], axis=0)
+
+
+def pack_probs(key_rows, query_rot, allowed):
+    scores = jnp.where(allowed, dot(key_rows, query_rot) * score_scale, masked_score)
+    exps = jnp.exp(scores - jnp.max(scores, axis=0, keepdims=True))
+    return exps / jnp.sum(exps, axis=0, keepdims=True)
+
+
+def pack_of(ref, p):
+    v = ref[lax.div(p, 2), lax.rem(p, 2)]
+    return v.reshape(SEQ, v.shape[-1])
+
+
+def attention_forward(x, cot, front, segs, gain_one, gain_two, gain_query, gain_key, table, cid):
+    def kernel(x, cot, front, segs, gain_one, gain_two, gain_query, gain_key, table,
+               a_full, cot_full, n_full, front_full, qk_pre, v_rows, mixed, middle,
+               shard, shard_two, a_buf, part, sibs, t, r, send, recv, lsem):
+        me = Place()
+
+        def norm_one(s):
+            v = x[s].astype(f32)
+            inverse = lax.rsqrt(jnp.mean(v * v, axis=-1, keepdims=True) + epsilon)
+            shard[s] = (v * inverse * gain_one[...]).astype(bf16)
+        chunks(128, norm_one)
+        meet([me.step("x", 1), me.step("x", -1), me.step("y", 1), me.step("y", -1),
+              me.step("z", 1), me.step("z", -1), me.sibling()])
+        w = Wire(send, recv)
+        locals_ = [pltpu.make_async_copy(front, front_full.at[me.x, me.y], lsem.at[0]),
+                   pltpu.make_async_copy(shard, a_buf.at[me.h, me.c, me.l], lsem.at[1]),
+                   pltpu.make_async_copy(cot, cot_full.at[me.h, me.c, me.l], lsem.at[2])]
+        gens = ag_xy_gens(w, me, front, front_full) + [ag_z_gen(w, me, shard, a_buf)]
+        for g in gens:
+            next(g)
+        for c in locals_:
+            c.start()
+        for c in locals_:
+            c.wait()
+        run(gens)
+        cot_gen = ag_z_gen(w, me, cot, cot_full)
+        next(cot_gen)
+        keep = pltpu.make_async_copy(a_buf, a_full, lsem.at[4])
+        keep.start()
+
+        def one_pack(p, _):
+            allowed, cosine, sine = pack_tables(segs, p, table)
+            weights = front_full[...].reshape(D, 640)
+            qkv = dot(pack_of(a_buf, p), weights[:, 0:384]).T
+            qk_pre[p] = qkv[0:320]
+            value = qkv[320:384].astype(bf16)
+            v_rows[p] = value
+            kn, _i = head_norm(qkv[256:320], gain_key[...])
+            key_rows = turn(kn, cosine, sine).T.astype(bf16)
+            heads = []
+            for j in range(4):
+                qn, _i = head_norm(qkv[64 * j:64 * j + 64], gain_query[...])
+                probs = pack_probs(key_rows, turn(qn, cosine, sine).astype(bf16), allowed)
+                heads.append(dot(value, probs.astype(bf16)))
+            o = jnp.concatenate(heads, axis=0).T.astype(bf16)
+            mixed[p] = o
+            out = dot(o, weights[:, 384:640], 1, 1).astype(bf16)
+            part[lax.div(p, 2), lax.rem(p, 2)] = out.reshape(2, 128, D)
+            return 0
+        lax.fori_loop(0, PACKS, one_pack, 0)
+        next(cot_gen)
+
+        def residual(s, v):
+            middle[s] = x[s].astype(f32) + v
+        run([rs_z_gen(w, me, part, residual, sibs, t, r)])
+
+        def norm_two(s):
+            v = middle[s]
+            inverse = lax.rsqrt(jnp.mean(v * v, axis=-1, keepdims=True) + epsilon)
+            shard_two[s] = (v * inverse * gain_two[...]).astype(bf16)
+        chunks(128, norm_two)
+        n_gen = ag_z_gen(w, me, shard_two, n_full)
+        next(n_gen)
+        own = pltpu.make_async_copy(shard_two, n_full.at[me.h, me.c, me.l], lsem.at[3])
+        own.start()
+        run([cot_gen])
+        run([n_gen])
+        own.wait()
+        keep.wait()
+        w.finish()
+
+    full = jax.ShapeDtypeStruct((2, 2, 2, 128, D), bf16)
+    return pl.pallas_call(
+        kernel,
+        out_shape=[full, full, full, jax.ShapeDtypeStruct((4, 4, 128, 640), bf16),
+                   jax.ShapeDtypeStruct((PACKS, 320, SEQ), f32), jax.ShapeDtypeStruct((PACKS, HD, SEQ), bf16),
+                   jax.ShapeDtypeStruct((PACKS, SEQ, 256), bf16), jax.ShapeDtypeStruct((128, D), f32)],
+        in_specs=vm_specs(9), out_specs=any_specs(3) + vm_specs(5),
+        scratch_shapes=[VM((128, D), bf16)] * 2 + [VM((2, 2, 2, 128, D), bf16)] * 2 + rs_z_scratch(D)
+        + dma_sems(64) + [pltpu.SemaphoreType.DMA((5,))],
+        compiler_params=params(cid))(x, cot, front, segs, gain_one, gain_two, gain_query, gain_key, table)
+
+
+def sigmoid(v):
+    return 1.0 / (1.0 + jnp.exp(-v))
+
+
+def feed_forward(n_full, cot_full, weights, cid):
+    def kernel(n_hbm, cot_hbm, w_hbm, grad_hbm, out_part, db_sum,
+               n, cot, w, hidden, gate_up, part, grad, sibs, t, r, send, recv, lsem, gsem):
+        me = Place()
+        loads = [pltpu.make_async_copy(n_hbm, n, lsem.at[0])]
+        loads += [pltpu.make_async_copy(w_hbm.at[:, pl.ds(1024 * i, 1024)], w.at[:, pl.ds(1024 * i, 1024)],
+                                        lsem.at[1 + i]) for i in range(3)]
+        loads.append(pltpu.make_async_copy(cot_hbm, cot, lsem.at[4]))
+        for c in loads:
+            c.start()
+        meet([me.step("z", 1), me.step("z", -1), me.sibling()])
+        for c in loads:
+            c.wait()
+
+        def hidden_block(i, _):
+            at = pl.multiple_of(i * 256, 256)
+            rows = n[...].reshape(ROWS, D)
+            g = dot(rows, w[:, pl.ds(at, 256)])
+            u = dot(rows, w[:, pl.ds(at + 1024, 256)])
+            dh = dot(cot[...].reshape(ROWS, D), w[:, pl.ds(at + 2048, 256)])
+            s = sigmoid(g)
+            silu = g * s
+            hidden[:, pl.ds(at, 256)] = (silu * u).astype(bf16)
+            gate_up[:, pl.ds(at, 256)] = (dh * u * (s + silu * (1.0 - s))).astype(bf16)
+            gate_up[:, pl.ds(at + 1024, 256)] = (dh * silu).astype(bf16)
+            return 0
+        lax.fori_loop(0, 4, hidden_block, 0)
+
+        def back_block(i, _):
+            at = pl.multiple_of(i * 256, 256)
+            v = dot(gate_up[...], w[pl.ds(at, 256), 0:2048], 1, 1).astype(bf16)
+            part[:, :, :, :, pl.ds(at, 256)] = v.reshape(2, 2, 2, 128, 256)
+            return 0
+        lax.fori_loop(0, 8, back_block, 0)
+        wire = Wire(send, recv)
+
+        def put(s, v):
+            db_sum[s] = v
+        gen = rs_z_gen(wire, me, part, put, sibs, t, r)
+        next(gen)
+        stores = []
+        for i in range(4):
+            at = 512 * i
+            slot = i % 2
+            if i >= 2:
+                stores[i - 2].wait()
+            grad[slot, :, 0:2048] = dot(n[:, :, :, :, at:at + 512].reshape(ROWS, 512), gate_up[...], 0, 0).astype(bf16)
+            grad[slot, :, 2048:3072] = dot(cot[:, :, :, :, at:at + 512].reshape(ROWS, 512), hidden[...], 0, 0).astype(bf16)
+            c = pltpu.make_async_copy(grad.at[slot], grad_hbm.at[pl.ds(at, 512)], gsem.at[i])
+            c.start()
+            stores.append(c)
+            if i == 0 or i == 2:
+                next(gen)
+
+        def out_block(i, _):
+            at = pl.multiple_of(i * 256, 256)
+            v = dot(hidden[...], w[pl.ds(at, 256), 2048:3072], 1, 1).astype(bf16)
+            out_part[:, :, :, :, pl.ds(at, 256)] = v.reshape(2, 2, 2, 128, 256)
+            return 0
+        lax.fori_loop(0, 8, out_block, 0)
+        run([gen])
+        stores[2].wait()
+        stores[3].wait()
+        wire.finish()
+
+    full = (2, 2, 2, 128, D)
+    return pl.pallas_call(
+        kernel,
+        out_shape=[jax.ShapeDtypeStruct((D, 3072), bf16), jax.ShapeDtypeStruct(full, bf16),
+                   jax.ShapeDtypeStruct((128, D), f32)],
+        in_specs=any_specs(3), out_specs=any_specs(1) + vm_specs(2),
+        scratch_shapes=[VM(full, bf16), VM(full, bf16), VM((D, 3072), bf16), VM((ROWS, 1024), bf16),
+                        VM((ROWS, 2048), bf16), VM(full, bf16), VM((2, 512, 3072), bf16)]
+        + rs_z_scratch(D) + dma_sems(16) + [pltpu.SemaphoreType.DMA((5,)), pltpu.SemaphoreType.DMA((4,))],
+        compiler_params=params(cid, 60))(n_full, cot_full, weights)
+
+
+def attention_backward(x, cot, middle, db_sum, out_part, a_full, front_full, qk_pre, v_rows, mixed, segs,
+                       gain_one, gain_two, gain_query, gain_key, table, cid):
+    def kernel(x, cot, middle, db_sum, out_part, a_full, front_full, qk_pre, v_rows, mixed, segs,
+               gain_one, gain_two, gain_query, gain_key, table,
+               input_grad, block_output, front_mine, gains,
+               shard, dm_full, mid_grad, dqkv, part, front_grad, q_acc, k_acc, one_acc, two_acc,
+               sibs_a, t_a, r_a, sibs_b, t_b, r_b, t1, r1, t2, r2, mid, send, recv, lsem):
+        me = Place()
+        two_acc[...] = jnp.zeros_like(two_acc)
+        one_acc[...] = jnp.zeros_like(one_acc)
+        q_acc[...] = jnp.zeros_like(q_acc)
+        k_acc[...] = jnp.zeros_like(k_acc)
+
+        def back(z, gain, up):
+            inverse = lax.rsqrt(jnp.mean(z * z, axis=-1, keepdims=True) + epsilon)
+            scaled = up * gain
+            inner = jnp.mean(z * scaled, axis=-1, keepdims=True)
+            return inverse * (scaled - z * inverse * inverse * inner), up * z * inverse
+
+        def norm_two(s):
+            dz, terms = back(middle[s], gain_two[...], db_sum[s])
+            v = cot[s].astype(f32) + dz
+            mid_grad[s] = v
+            shard[s] = v.astype(bf16)
+            two_acc[...] += terms
+        chunks(128, norm_two)
+        meet([me.step("x", 1), me.step("x", -1), me.step("y", 1), me.step("y", -1),
+              me.step("z", 1), me.step("z", -1), me.sibling()])
+        w = Wire(send, recv)
+        gen = ag_z_gen(w, me, shard, dm_full)
+        next(gen)
+        own = pltpu.make_async_copy(shard, dm_full.at[me.h, me.c, me.l], lsem.at[0])
+        own.start()
+        run([gen])
+        own.wait()
+
+        def put_out(s, v):
+            block_output[s] = middle[s] + v
+        out_gen = rs_z_gen(w, me, out_part, put_out, sibs_a, t_a, r_a)
+        next(out_gen)
+
+        def one_pack(p, _):
+            allowed, cosine, sine = pack_tables(segs, p, table)
+            weights = front_full[...].reshape(D, 640)
+            mixed_grad = dot(pack_of(dm_full, p), weights[:, 384:640]).T.astype(bf16)
+            value_rows = v_rows[p].astype(f32).T.astype(bf16)
+            key_pre = qk_pre[p, 256:320]
+            kn, k_inverse = head_norm(key_pre, gain_key[...])
+            kr = turn(kn, cosine, sine)
+            key_rows = kr.T.astype(bf16)
+            kr = kr.astype(bf16)
+            dk = jnp.zeros((HD, SEQ), f32)
+            dv = jnp.zeros((HD, SEQ), f32)
+            heads = []
+            terms_q = jnp.zeros((HD, SEQ), f32)
+            for j in range(4):
+                query_pre = qk_pre[p, 64 * j:64 * j + 64]
+                qn, q_inverse = head_norm(query_pre, gain_query[...])
+                qr = turn(qn, cosine, sine).astype(bf16)
+                probs = pack_probs(key_rows, qr, allowed)
+                do = mixed_grad[64 * j:64 * j + 64]
+                dp = dot(value_rows, do)
+                inner = jnp.sum(probs * dp, axis=0, keepdims=True)
+                ds = (probs * (dp - inner)).astype(bf16)
+                dqr = dot(kr, ds) * score_scale
+                dk += dot(qr, ds, 1, 1)
+                dv += dot(do, probs.astype(bf16), 1, 1)
+                dq, terms = head_norm_back(query_pre, q_inverse, gain_query[...], turn_back(dqr, cosine, sine))
+                terms_q += terms
+                heads.append(dq)
+            dk, terms_k = head_norm_back(key_pre, k_inverse, gain_key[...], turn_back(dk * score_scale, cosine, sine))
+            q_acc[...] += terms_q
+            k_acc[...] += terms_k
+            grads = jnp.concatenate(heads + [dk, dv], axis=0).T.astype(bf16)
+            dqkv[p] = grads
+            out = dot(grads, weights[:, 0:384], 1, 1).astype(bf16)
+            part[lax.div(p, 2), lax.rem(p, 2)] = out.reshape(2, 128, D)
+            return 0
+        lax.fori_loop(0, 2, one_pack, 0)
+        next(out_gen)
+        lax.fori_loop(2, PACKS, one_pack, 0)
+        next(out_gen)
+        for i in range(4):
+            at = 512 * i
+            a_rows = a_full[:, :, :, :, at:at + 512].reshape(ROWS, 512)
+            dm_rows = dm_full[:, :, :, :, at:at + 512].reshape(ROWS, 512)
+            g = jnp.concatenate([dot(a_rows, dqkv[...].reshape(ROWS, 384), 0, 0),
+                                 dot(dm_rows, mixed[...].reshape(ROWS, 256), 0, 0)], axis=1)
+            front_grad[i] = g.astype(bf16).reshape(4, 128, 640)
+
+        def put_in(s, v):
+            dz, terms = back(x[s].astype(f32), gain_one[...], v)
+            input_grad[s] = mid_grad[s] + dz
+            one_acc[...] += terms
+        run([out_gen])
+        in_gen = rs_z_gen(w, me, part, put_in, sibs_b, t_b, r_b)
+        run([in_gen] + rs_xy_gens(w, me, front_grad, front_mine, t1, r1, t2, r2, mid))
+        w.finish()
+        one = jnp.sum(one_acc[...], axis=0, keepdims=True)
+        two = jnp.sum(two_acc[...], axis=0, keepdims=True)
+        for i in range(16):
+            gains[i:i + 1, :] = one[:, 128 * i:128 * i + 128]
+            gains[16 + i:17 + i, :] = two[:, 128 * i:128 * i + 128]
+        small = jnp.concatenate([q_acc[...], k_acc[...]], axis=0).T
+        gains[32:33, :] = jnp.sum(small, axis=0, keepdims=True)
+
+    full = (2, 2, 2, 128, D)
+    rows = jax.ShapeDtypeStruct((128, D), f32)
+    return pl.pallas_call(
+        kernel,
+        out_shape=[rows, rows, jax.ShapeDtypeStruct((128, 640), bf16), jax.ShapeDtypeStruct((33, 128), f32)],
+        in_specs=vm_specs(16), out_specs=vm_specs(4),
+        scratch_shapes=[VM((128, D), bf16), VM(full, bf16), VM((128, D), f32), VM((PACKS, SEQ, 384), bf16),
+                        VM(full, bf16), VM((4, 4, 128, 640), bf16), VM((HD, SEQ), f32), VM((HD, SEQ), f32),
+                        VM((16, D), f32), VM((16, D), f32)]
+        + rs_z_scratch(D) * 2 + rs_xy_scratch(640) + dma_sems(64) + [pltpu.SemaphoreType.DMA((2,))],
+        compiler_params=params(cid, 60))(
+            x, cot, middle, db_sum, out_part, a_full, front_full, qk_pre, v_rows, mixed, segs,
+            gain_one, gain_two, gain_query, gain_key, table)
+
+
+def adam(weight, moment, square, gradient, rate, decay):
+    momentum = beta_one * moment + (1.0 - beta_one) * gradient
+    variance = beta_two * square + (1.0 - beta_two) * gradient * gradient
+    ratio = momentum / (1.0 - beta_one**STEP) / (jnp.sqrt(variance / (1.0 - beta_two**STEP)) + adam_epsilon)
+    return weight - rate * (ratio + decay * weight), momentum, variance
+
+
+RATES = (0.04, 0.04, 0.04, 0.15, 0.04, 0.04, 0.02)
+SPANS = (256, 64, 64, 256, 1024, 1024, 1024)
+
+
+def update(front, rest, gain_terms, gain_states, states, cid):
+    def kernel(*refs):
+        front, rest, terms, g_w, g_m, g_v = refs[:6]
+        ins, g_out, outs = refs[6:27], refs[27:30], refs[30:51]
+        fbuf, rbuf, z_in, x_in, y_in = refs[51:56]
+        held, made = refs[56:77], refs[77:98]
+        send, recv, lsem, osem = refs[98:]
+        me = Place()
+        loads = [pltpu.make_async_copy(a, b, lsem.at[i]) for i, (a, b) in enumerate(zip(ins, held))]
+        for c in loads:
+            c.start()
+        peers = swap_devs(me)
+        mine = me.h * 2 + me.c
+        zs = [me.at(z=m4(me.z + dz), c=lax.rem(me.c + dc, 2)) for dz in range(4) for dc in range(2) if dz or dc]
+        xs = [me.step("x", d) for d in (1, 2, 3)]
+        ys = [me.step("y", d) for d in (1, 2, 3)]
+        meet(zs + xs + ys)
+        w = Wire(send, recv)
+
+        def total(buf, n):
+            v = buf[0]
+            for k in range(1, n):
+                v = v + buf[k]
+            return v
+
+        def share(value, buf, slot, devs):
+            buf[slot] = value
+            return [w.go(buf.at[slot], buf.at[slot], d) for d in devs]
+        gs = share(terms[...], z_in, me.z * 2 + me.c, zs)
+        arrivals = []
+        for j, dev in reversed(peers):
+            arrivals.append(w.go(front.at[j], fbuf.at[mine], dev))
+            arrivals.append(w.go(rest.at[j], rbuf.at[mine], dev))
+        fbuf[mine] = front[mine]
+        rbuf[mine] = rest[mine]
+        for c in gs:
+            c.wait_recv()
+        gs = share(total(z_in, 8), x_in, me.x, xs)
+        for c in gs:
+            c.wait_recv()
+        gs = share(total(x_in, 4), y_in, me.y, ys)
+        for c in gs:
+            c.wait_recv()
+        new = adam(g_w[...], g_m[...], g_v[...], total(y_in, 4), gain_rate, 0.0)
+        for ref, v in zip(g_out, new):
+            ref[...] = v
+        for c in loads:
+            c.wait()
+        for a in arrivals:
+            a.wait_recv()
+        stores = []
+        at = {False: 0, True: 0}
+        for i, (n, rate) in enumerate(zip(SPANS, RATES)):
+            late = i >= 4
+            buf = rbuf if late else fbuf
+            for j in range(4):
+                here = pl.ds(n * j, n)
+                grad = buf[j, :, at[late]:at[late] + n].astype(f32)
+                new = adam(held[3 * i][:, here], held[3 * i + 1][:, here], held[3 * i + 2][:, here], grad, rate,
+                           weight_decay)
+                for k in range(3):
+                    made[3 * i + k][:, here] = new[k]
+            at[late] += n
+            for k in range(3):
+                c = pltpu.make_async_copy(made[3 * i + k], outs[3 * i + k], osem.at[3 * i + k])
+                c.start()
+                stores.append(c)
+        for c in stores:
+            c.wait()
+        w.finish()
+
+    shapes = [jax.ShapeDtypeStruct(s.shape, f32) for s in states]
+    gain_shape = jax.ShapeDtypeStruct((33, 128), f32)
+    return pl.pallas_call(
+        kernel, out_shape=[gain_shape] * 3 + shapes,
+        in_specs=vm_specs(6) + any_specs(21), out_specs=vm_specs(3) + any_specs(21),
+        scratch_shapes=[VM((4, 32, 640), bf16), VM((4, 32, 3072), bf16), VM((8, 33, 128), f32), VM((4, 33, 128), f32),
+                        VM((4, 33, 128), f32)] + [VM(s.shape, f32) for s in states] * 2
+        + dma_sems(19) + [pltpu.SemaphoreType.DMA((21,)), pltpu.SemaphoreType.DMA((21,))],
+        compiler_params=params(cid))(front, rest, gain_terms, *gain_states, *states)
+
+
+from jax.sharding import PartitionSpec as P
+
 PLANE = [[x * 16 + y * 4 + k for x in range(4) for y in range(4)] for k in range(4)]
-
-
-def rows_product(left, right):
-    return lax.dot_general(left, right, (((0,), (0,)), ((), ())), preferred_element_type=f32)
-
-
-def column_product(left, right):
-    return lax.dot_general(left, right, (((1,), (1,)), ((), ())), preferred_element_type=f32)
-
-
-def product(left, right):
-    return jnp.dot(left, right, preferred_element_type=f32)
-
-
-def norm_forward(values, gain):
-    inverse = lax.rsqrt(jnp.mean(values * values, axis=-1, keepdims=True) + epsilon)
-    return (values * inverse * gain, inverse)
-
-
-def norm_backward(values, inverse, gain, upstream):
-    scaled = upstream * gain
-    inner = jnp.mean(values * scaled, axis=-1, keepdims=True)
-    return (inverse * (scaled - values * inverse * inverse * inner), upstream * values * inverse)
-
-
-def positions_of(rows):
-    places = jnp.arange(SEQ, dtype=jnp.int32)[None, :]
-    fresh = jnp.concatenate([jnp.ones((rows.shape[0], 1), jnp.bool_), rows[:, 1:] != rows[:, :-1]], axis=1)
-    starts = jnp.where(fresh, places, 0)
-    return places - lax.cummax(starts, axis=1)
-
-
-def rope_tables(positions):
-    half_dim = HD // 2
-    frequency = rope_base ** (-2.0 * jnp.arange(half_dim, dtype=f32) / HD)
-    angles = positions.astype(f32)[..., None] * frequency
-    return (jnp.cos(angles), jnp.sin(angles))
-
-
-def rotate(values, cosine, sine):
-    front, back = values[..., : HD // 2], values[..., HD // 2 :]
-    return jnp.concatenate([front * cosine - back * sine, back * cosine + front * sine], axis=-1)
-
-
-def adam_step(weights_now, moment_now, square_now, gradient, step_rate, decay_rate):
-    momentum = beta_one * moment_now + (1.0 - beta_one) * gradient
-    variance = beta_two * square_now + (1.0 - beta_two) * gradient * gradient
-    ratio = momentum / (1.0 - beta_one**STEP) / (jnp.sqrt(variance / (1.0 - beta_two**STEP)) + adam_epsilon)
-    return (weights_now - step_rate * (ratio + decay_rate * weights_now), momentum, variance)
-
-
-def split_out(parts):
-    return jnp.concatenate([p.reshape(32, 4, -1) for p in parts], axis=2).transpose(1, 0, 2)
-
-
-def join_back(whole, widths):
-    out, at = [], 0
-    for n in widths:
-        out.append(whole[:, :, at : at + n].transpose(1, 0, 2).reshape(32, 4 * n))
-        at += n
-    return out
 
 
 def gather_plane(shard):
@@ -550,128 +985,26 @@
     return lax.psum_scatter(whole, "dp", axis_index_groups=PLANE, scatter_dimension=0, tiled=True)
 
 
-def gather_tokens(shard):
-    return ag_z(shard, 3).reshape(ROWS, D)
-
-
-def scatter_tokens(whole):
-    return rs_z(whole.astype(bf16).reshape(2, 2, 2, 128, D), 4)
-
-
-def local(
-    block_input, output_grad, segment_ids, norm_gains, gain_moment, gain_square,
-    query_weight, query_moment, query_square, key_weight, key_moment, key_square,
-    value_weight, value_moment, value_square, output_weight, output_moment, output_square,
-    gate_weight, gate_moment, gate_square, up_weight, up_moment, up_square,
-    down_weight, down_moment, down_square,
-):
-    gain_one = norm_gains[:D]
-    gain_two = norm_gains[D : 2 * D]
-    gain_query = norm_gains[2 * D : 2 * D + HD]
-    gain_key = norm_gains[2 * D + HD :]
-    low = lambda w: w.astype(bf16)
-    front_out = split_out([low(query_weight), low(key_weight), low(value_weight), low(output_weight)])
-    rest_out = split_out([low(gate_weight), low(up_weight), low(down_weight)])
-    segment_out = jnp.broadcast_to(segment_ids[None], (4, 8, SEQ))
-    front_shard, rest_shard, segments = swap_hc([front_out, rest_out, segment_out], 1)
-    front_full = gather_plane(front_shard.reshape(128, 640))
+def local(block_input, output_grad, segment_ids, norm_gains, gain_moment, gain_square, *states):
+    gain_one = norm_gains[:D][None]
+    gain_two = norm_gains[D : 2 * D][None]
+    gain_query = norm_gains[2 * D : 2 * D + HD][:, None]
+    gain_key = norm_gains[2 * D + HD :][:, None]
+    table = jnp.asarray(rope_constants())
+    front_shard, rest_shard, segments = spread_weights(states[::3], segment_ids, 1)
     rest_full = gather_plane(rest_shard.reshape(128, 3072))
-    qkv_full, output_full = front_full[:, :384], front_full[:, 384:]
-    gate_up_full, down_full = rest_full[:, :2048], rest_full[:, 2048:]
-
-    rows_in = block_input.astype(f32)
-    normed_one, inverse_one = norm_forward(rows_in, gain_one)
-    gathered_one = gather_tokens(normed_one.astype(bf16))
-    gathered_cot = gather_tokens(output_grad)
-
-    packs = segments[:, 0, :]
-    cosine, sine = rope_tables(positions_of(packs))
-    places = jnp.arange(SEQ, dtype=jnp.int32)
-    allowed = (packs[:, :, None] == packs[:, None, :]) & (places[None, None, :] <= places[None, :, None])
-    score_scale = HD ** (-0.5)
-
-    qkv = product(gathered_one, qkv_full)
-    query_pre = qkv[:, :256].reshape(PACKS, SEQ, 4, HD)
-    key_pre = qkv[:, 256:320].reshape(PACKS, SEQ, HD)
-    value_low = qkv[:, 320:].astype(bf16).reshape(PACKS, SEQ, HD)
-    query_normed, query_inverse = norm_forward(query_pre, gain_query)
-    key_normed, key_inverse = norm_forward(key_pre, gain_key)
-    query_rot = rotate(query_normed, cosine[:, :, None, :], sine[:, :, None, :]).astype(bf16)
-    key_rot = rotate(key_normed, cosine, sine).astype(bf16)
-    scores = jnp.einsum("pqjd,pkd->pjqk", query_rot, key_rot, preferred_element_type=f32) * score_scale
-    scores = jnp.where(allowed[:, None], scores, masked_score)
-    exps = jnp.exp(scores - jnp.max(scores, axis=-1, keepdims=True))
-    probs = exps / jnp.sum(exps, axis=-1, keepdims=True)
-    probs_low = probs.astype(bf16)
-    mixed = jnp.einsum("pjqk,pkd->pqjd", probs_low, value_low, preferred_element_type=f32)
-    mixed_low = mixed.astype(bf16).reshape(ROWS, 256)
-
-    middle = rows_in + scatter_tokens(column_product(mixed_low, output_full))
-    normed_two, inverse_two = norm_forward(middle, gain_two)
-    gathered_two = gather_tokens(normed_two.astype(bf16))
-    gate_up = product(gathered_two, gate_up_full)
-    gate_pre, up_pre = gate_up[:, :1024], gate_up[:, 1024:]
-    sigmoid_gate = jax.nn.sigmoid(gate_pre)
-    silu_gate = gate_pre * sigmoid_gate
-    hidden_low = (silu_gate * up_pre).astype(bf16)
-
-    hidden_grad = product(gathered_cot, down_full)
-    up_low = (hidden_grad * silu_gate).astype(bf16)
-    gate_low = (hidden_grad * up_pre * (sigmoid_gate + silu_gate * (1.0 - sigmoid_gate))).astype(bf16)
-    gate_up_low = jnp.concatenate([gate_low, up_low], axis=1)
-    gate_up_grad = rows_product(gathered_two, gate_up_low)
-    down_grad = rows_product(gathered_cot, hidden_low)
-    rest_grad = jnp.concatenate([gate_up_grad.astype(bf16), down_grad.astype(bf16)], axis=1)
+    one_full, cot_full, two_full, front_full, qk_pre, v_rows, mixed, middle = attention_forward(
+        block_input, output_grad, front_shard.reshape(128, 640), segments, gain_one, gain_two, gain_query, gain_key,
+        table, 2)
+    rest_grad, out_part, db_sum = feed_forward(two_full, cot_full, rest_full, 3)
     rest_mine = scatter_plane(rest_grad)
-
-    normed_two_grad = scatter_tokens(column_product(gate_up_low, gate_up_full))
-    block_output = middle + scatter_tokens(column_product(hidden_low, down_full))
-    middle_back, gain_two_terms = norm_backward(middle, inverse_two, gain_two, normed_two_grad)
-    middle_grad = output_grad.astype(f32) + middle_back
-    gathered_attn = gather_tokens(middle_grad.astype(bf16))
-    mixed_grad = product(gathered_attn, output_full).astype(bf16).reshape(PACKS, SEQ, 4, HD)
-    output_weight_grad = rows_product(gathered_attn, mixed_low)
-
-    prob_grad = jnp.einsum("pqjd,pkd->pjqk", mixed_grad, value_low, preferred_element_type=f32)
-    inner_term = jnp.sum(probs * prob_grad, axis=-1, keepdims=True)
-    score_grad = (probs * (prob_grad - inner_term)).astype(bf16)
-    query_rot_grad = jnp.einsum("pjqk,pkd->pqjd", score_grad, key_rot, preferred_element_type=f32) * score_scale
-    key_rot_grad = jnp.einsum("pjqk,pqjd->pkd", score_grad, query_rot, preferred_element_type=f32) * score_scale
-    value_grad = jnp.einsum("pjqk,pqjd->pkd", probs_low, mixed_grad, preferred_element_type=f32).astype(bf16)
-    query_pre_grad, gain_query_terms = norm_backward(
-        query_pre, query_inverse, gain_query, rotate(query_rot_grad, cosine[:, :, None, :], -sine[:, :, None, :])
-    )
-    key_pre_grad, gain_key_terms = norm_backward(key_pre, key_inverse, gain_key, rotate(key_rot_grad, cosine, -sine))
-    qkv_low = jnp.concatenate(
-        [query_pre_grad.astype(bf16).reshape(ROWS, 256), key_pre_grad.astype(bf16).reshape(ROWS, HD),
-         value_grad.reshape(ROWS, HD)], axis=1
-    )
-    qkv_grad = rows_product(gathered_one, qkv_low)
-    front_grad = jnp.concatenate([qkv_grad.astype(bf16), output_weight_grad.astype(bf16)], axis=1)
-    front_mine = scatter_plane(front_grad)
-    normed_one_grad = scatter_tokens(column_product(qkv_low, qkv_full))
-    input_back, gain_one_terms = norm_backward(rows_in, inverse_one, gain_one, normed_one_grad)
-    input_grad = middle_grad + input_back
-
-    gain_local = jnp.concatenate(
-        [jnp.sum(gain_one_terms, axis=0), jnp.sum(gain_two_terms, axis=0),
-         jnp.sum(gain_query_terms, axis=(0, 1, 2)), jnp.sum(gain_key_terms, axis=(0, 1))]
-    )
-    gain_grads = sum_all(gain_local.reshape(33, 128), 5).reshape(-1)
-
-    front_back, rest_back = swap_hc([front_mine.reshape(4, 32, 640), rest_mine.reshape(4, 32, 3072)], 2)
-    sums = join_back(front_back.astype(f32), (256, 64, 64, 256)) + join_back(rest_back.astype(f32), (1024, 1024, 1024))
-    results = [block_output, input_grad]
-    results += adam_step(norm_gains, gain_moment, gain_square, gain_grads, gain_rate, 0.0)
-    states = (
-        (query_weight, query_moment, query_square, 0.04), (key_weight, key_moment, key_square, 0.04),
-        (value_weight, value_moment, value_square, 0.04), (output_weight, output_moment, output_square, 0.15),
-        (gate_weight, gate_moment, gate_square, 0.04), (up_weight, up_moment, up_square, 0.04),
-        (down_weight, down_moment, down_square, 0.02),
-    )
-    for (w, m, v, rate), grad in zip(states, sums):
-        results += adam_step(w, m, v, grad, rate, weight_decay)
-    return tuple(results)
+    input_grad, block_output, front_mine, gain_terms = attention_backward(
+        block_input, output_grad, middle, db_sum, out_part, one_full, front_full, qk_pre, v_rows, mixed, segments,
+        gain_one, gain_two, gain_query, gain_key, table, 4)
+    square = lambda v: v.reshape(33, 128)
+    news = update(front_mine.reshape(4, 32, 640), rest_mine.reshape(4, 32, 3072), gain_terms,
+                  [square(norm_gains), square(gain_moment), square(gain_square)], states, 5)
+    return (block_output, input_grad) + tuple(v.reshape(-1) for v in news[:3]) + tuple(news[3:])
 
 
 def solution(mesh):

time: 533 us -> 350 us (0.66); the launches traced: 523 us -> 349 us
  matrix products: 101 us -> 0 us
  other arithmetic: 58.1 us -> 0 us
  Pallas kernels: 279 us -> 298 us
  local copies, waits for them, and re-layouts: 40.5 us -> 22.2 us
  waiting for transfers between devices: 28.2 us -> 13.8 us
    dot_general x17 -> x0, matrix products: 96.8 us -> none  [the longest x4 32.7 us: column_product(): lax.dot_general(left, right, (((1,), (1,)), ((), ())), preferred_element_...]
    pallas_call x11 -> x5, Pallas kernels: 279 us -> 298 us  [the longest x1 113 us: attention_forward(): pl.pallas_call(kernel, out_shape=[full, full, full, jax.ShapeDtypeStruct(...]
    concatenate x3 -> x0, other arithmetic: 17.1 us -> none  [the longest x1 14.9 us: local(): jnp.concatenate([gate_up_grad.astype(bf16), down_grad.astype(bf16)], axis=1)]
    convert_element_type x15 -> x0, other arithmetic: 14.3 us -> none  [the longest x7 6.63 us: local(): low = lambda w: w.astype(bf16)]
    reduce_scatter x2 -> x1, waiting for transfers between devices: 27.5 us -> 13.7 us  [scatter_plane(): lax.psum_scatter(whole, 'dp', axis_index_groups=PLANE, scatter_dimension=...]
    sub x9 -> x0, other arithmetic: 8.6 us -> none  [the longest x8 8.46 us: adam_step(): weights_now - step_rate * (ratio + decay_rate * weights_now)]
    reshape x20 -> x0, local copies, waits for them, and re-layouts: 8.03 us -> none  [the longest x2 4.93 us: local(): product(gathered_attn, output_full).astype(bf16).reshape(PACKS, SEQ, 4, HD)]
    unnamed x146 -> x78, local copies, waits for them, and re-layouts: 26.6 us -> 18.6 us
  transfers between devices with their start and end apart: 4 -> 2, of which waited for: 1 -> 1; matrix products, arithmetic and copies ran while one was open for 21% -> 1% of each run, Pallas kernels for 34% -> 57%
where the time goes in v2:
time: 350 us; the launch traced here: 349 us
  Pallas kernels  298 us (85%)
  local copies, waits for them, and re-layouts  22.2 us (6%)
  between operations  14.3 us (4%)
  waiting for transfers between devices  13.8 us (4%)
    pallas_call x1, Pallas kernels, attention_forward(): pl.pallas_call(kernel, out_shape=[full, full, full, jax.ShapeDtypeStruct(...  113 us
    pallas_call x1, Pallas kernels, attention_backward(): pl.pallas_call(kernel, out_shape=[rows, rows, jax.ShapeDtypeStruct((128,...  84.8 us
    pallas_call x1, Pallas kernels, feed_forward(): pl.pallas_call(kernel, out_shape=[jax.ShapeDtypeStruct((D, 3072), bf16),...  58.8 us
    pallas_call x1, Pallas kernels, update(): pl.pallas_call(kernel, out_shape=[gain_shape] * 3 + shapes, in_specs=vm_s...  22 us
    pallas_call x1, Pallas kernels, spread_weights(): pl.pallas_call(kernel, out_shape=[jax.ShapeDtypeStruct((4, 32, 640), bf16...  19.5 us
    unnamed x78, local copies, waits for them, and re-layouts  18.6 us
    reduce_scatter x1, waiting for transfers between devices, scatter_plane(): lax.psum_scatter(whole, 'dp', axis_index_groups=PLANE, scatter_dimension=...  13.7 us
  transfers between devices with their start and end apart: 2, of which 1 were waited for; matrix products, arithmetic and copies ran while one was open for 1% of the time, Pallas kernels for 57%

profile of v2, /device:TPU:1, one launch (start us, length us, event | category | flops | bytes accessed | tf_op | source)
XLA Modules:
  0.0 348.7 jit_solution(2354211288598042607)
XLA Ops:
  7.2 0.0 all-gather.2.cloned.1.call-start
  7.2 19.5 %shard_map.467 = (bf16[4,32,640]{2,1,0:T(8,128)(2,1)}, bf16[4,32,3072]{2,1,0:T(8,128)(2,1)}, s32[4,8,256]{2,1,0:T(8,128)}) custom-call(f32[32,1024]{1,0:T(8,128)} %refs_6_.1, f32[32,256]{1,0:T(8,128)} %refs_9_.1, f32[32,256]{1,0:T(8,128)} %refs_12_.1, f32[32,1024]{1,0:T(8,128)} %refs_15_.1, f32[32,4096]{1,0:T(8,128)} %refs_18_.1, f32[32,4096]{1,0:T(8,128)} %refs_21_.1, ...), custom_call_target="tpu_custom_call" | custom-call | tf_op jit(solution)/shard_map/pallas_call | solution.py:537
  26.8 0.0 all-gather.2.cloned.1.call-update
  26.8 0.0 reduce-scatter.2.cloned.1.call-start
  26.8 0.8 slice_bitcast_fusion
  27.7 0.7 copy.55.gain_key
  28.4 0.7 copy.54.gain_query
  29.1 1.3 fusion
  30.4 113.2 %shard_map.468 = (bf16[2,2,2,128,2048]{4,3,2,1,0:T(8,128)(2,1)}, bf16[2,2,2,128,2048]{4,3,2,1,0:T(8,128)(2,1)}, bf16[2,2,2,128,2048]{4,3,2,1,0:T(8,128)(2,1)}, b...) custom-call(bf16[128,2048]{1,0:T(8,128)(2,1)} %x.3, ...), custom_call_target="tpu_custom_call" | custom-call | tf_op jit(solution)/shard_map/pallas_call | solution.py:669
  143.7 0.0 all-gather.2.cloned.1.call-done.w_hbm
  143.7 58.8 %shard_map.469 = (bf16[2048,3072]{1,0:T(8,128)(2,1)}, bf16[2,2,2,128,2048]{4,3,2,1,0:T(8,128)(2,1)}, f32[128,2048]{1,0:T(8,128)}) custom-call(bf16[2,2,2,128,2048]{4,3,2,1,0:T(8,128)(2,1)} %get-tuple-element.71.n_hbm, bf16[2,2,2,128,2048]{4,3,2,1,0:T(8,128)(2,1)} %get-tuple-element.72.cot_hbm, bf16[2048,3072]{1,0:T(8,128)(2,1)} %all-gather.2.cloned.1.call-done.w_hbm), custom_call_target="tpu_custom_call" | custom-call | tf_op jit(solution)/shard_map/pallas_call | solution.py:750
  202.5 0.0 reduce-scatter.2.cloned.1.call-update
  202.5 84.8 %shard_map.470 = (f32[128,2048]{1,0:T(8,128)}, f32[128,2048]{1,0:T(8,128)}, bf16[128,640]{1,0:T(8,128)(2,1)}, f32[33,128]{1,0:T(8,128)}) custom-call(bf16[128,2048]{1,0:T(8,128)(2,1)} %x.3, bf16[128,2048]{1,0:T(8,128)(2,1)} %cot.3, f32[128,2048]{1,0:T(8,128)} %get-tuple-element.70.middle, f32[128,2048]{1,0:T(8,128)} %get-tuple-element.74.db_sum, ...), custom_call_target="tpu_custom_call" | custom-call | tf_op jit(solution)/shard_map/pallas_call | solution.py:869
  287.3 0.0 copy-start.1
  287.3 13.7 %reduce-scatter.2.cloned.1.call-done = bf16[128,3072]{1,0:T(8,128)(2,1)} async-done(((bf16[2048,3072]{1,0:T(8,128)(2,1)}), bf16[128,3072]{1,0:T(8,128)(2,1)}) %reduce-scatter.2.cloned.1.call-update) | async-done | bytes 786448 | tf_op jit(solution)/shard_map/reduce_scatter | solution.py:985
  301.0 22.0 %shard_map.471 = (f32[33,128]{1,0:T(8,128)}, f32[33,128]{1,0:T(8,128)}, f32[33,128]{1,0:T(8,128)}, f32[32,1024]{1,0:T(8,128)}, f32[32,1024]{1,0:T(8,128)}, /*ind...) custom-call(bf16[4,32,640]{2,1,0:T(8,128)(2,1)} %bitcast.18, ...), custom_call_target="tpu_custom_call" | custom-call | tf_op jit(solution)/shard_map/pallas_call | solution.py:966
  323.1 0.0 copy-start.25
  323.1 0.0 copy-start.24
  323.1 0.0 copy-start.23
  323.1 0.0 copy-start.16
  323.1 0.0 copy-start.15
  323.1 0.0 copy-start.14
  323.1 0.0 copy-start.22
  323.1 0.0 copy-start.21
  323.1 0.0 copy-start.20
  323.1 0.0 copy-start.19
  323.2 0.0 copy-start.18
  323.2 0.0 copy-start.17
  323.2 0.0 copy-start.13
  323.2 0.0 copy-start.12
  323.2 0.0 copy-start.11
  323.2 0.0 copy-start.10
  323.2 0.0 copy-start.9
  323.2 0.0 copy-start.8
  323.2 0.0 copy-done.1
  323.3 1.0 copy.84
  324.2 0.0 copy-done
  324.2 1.0 copy.85
  325.2 0.6 copy.86
  325.8 0.6 copy.87
  326.4 0.6 copy.88
  327.1 0.7 copy.89
  327.7 0.7 copy.90
  328.4 0.7 copy.91
  329.0 0.6 copy.92
  329.6 0.6 copy.93
  330.3 0.6 copy.94
  330.9 0.6 copy.95
  331.5 0.0 copy-done.18
  331.5 0.6 copy.96
  332.1 0.6 copy.97
  332.7 0.7 copy.98
  333.4 0.7 copy.99
  334.1 0.7 copy.100
  334.7 0.8 copy.101
  335.5 0.8 copy.102
  336.3 0.8 copy.103
  337.1 0.8 copy.104
  337.9 0.0 copy-done.6
  337.9 0.8 copy.105
  338.7 0.8 copy.106
  339.5 0.8 copy.107
  340.3 0.8 copy.108
  341.1 0.8 copy.109
  (29 shorter events, 0.1 us)
Async XLA Ops:
  7.2 136.5 %all-gather.2.cloned.1.call-start = ((), (), s32[]{:S(2)}) async-start(), calls=%async_computation.1 | async-start | bytes 13369344 | tf_op jit(solution)/shard_map/all_gather | solution.py:981
  26.8 274.2 %reduce-scatter.2.cloned.1.call-start = ((), (), s32[]{:S(2)}) async-start(), calls=%async_computation.2 | async-start | bytes 13369344 | tf_op jit(solution)/shard_map/reduce_scatter | solution.py:985
  287.3 36.0 %copy-start.1 = (f32[128,2048]{1,0:T(8,128)S(1)}, f32[128,2048]{1,0:T(8,128)}, u32[]{:S(2)}) copy-start(f32[128,2048]{1,0:T(8,128)} %get-tuple-element.140) | copy-start | bytes 3145732
  301.0 23.2 %copy-start = (f32[128,2048]{1,0:T(8,128)S(1)}, f32[128,2048]{1,0:T(8,128)}, u32[]{:S(2)}) copy-start(f32[128,2048]{1,0:T(8,128)} %get-tuple-element.141) | copy-start | bytes 3145732
  323.1 2.2 copy-start.25
  323.1 2.8 copy-start.24
  323.1 3.4 copy-start.23
  323.1 4.0 %copy-start.16 = (f32[32,1024]{1,0:T(8,128)S(1)}, f32[32,1024]{1,0:T(8,128)}, u32[]{:S(2)}) copy-start(f32[32,1024]{1,0:T(8,128)} %get-tuple-element.145) | copy-start | bytes 393220
  323.1 4.6 %copy-start.15 = (f32[32,1024]{1,0:T(8,128)S(1)}, f32[32,1024]{1,0:T(8,128)}, u32[]{:S(2)}) copy-start(f32[32,1024]{1,0:T(8,128)} %get-tuple-element.146) | copy-start | bytes 393220
  323.1 5.3 %copy-start.14 = (f32[32,1024]{1,0:T(8,128)S(1)}, f32[32,1024]{1,0:T(8,128)}, u32[]{:S(2)}) copy-start(f32[32,1024]{1,0:T(8,128)} %get-tuple-element.147) | copy-start | bytes 393220
  323.1 5.9 %copy-start.22 = (f32[32,256]{1,0:T(8,128)S(1)}, f32[32,256]{1,0:T(8,128)}, u32[]{:S(2)}) copy-start(f32[32,256]{1,0:T(8,128)} %get-tuple-element.148) | copy-start | bytes 98308
  323.1 6.5 %copy-start.21 = (f32[32,256]{1,0:T(8,128)S(1)}, f32[32,256]{1,0:T(8,128)}, u32[]{:S(2)}) copy-start(f32[32,256]{1,0:T(8,128)} %get-tuple-element.149) | copy-start | bytes 98308
  323.1 7.1 %copy-start.20 = (f32[32,256]{1,0:T(8,128)S(1)}, f32[32,256]{1,0:T(8,128)}, u32[]{:S(2)}) copy-start(f32[32,256]{1,0:T(8,128)} %get-tuple-element.150) | copy-start | bytes 98308
  323.1 7.7 %copy-start.19 = (f32[32,256]{1,0:T(8,128)S(1)}, f32[32,256]{1,0:T(8,128)}, u32[]{:S(2)}) copy-start(f32[32,256]{1,0:T(8,128)} %get-tuple-element.151) | copy-start | bytes 98308
  323.2 8.3 %copy-start.18 = (f32[32,256]{1,0:T(8,128)S(1)}, f32[32,256]{1,0:T(8,128)}, u32[]{:S(2)}) copy-start(f32[32,256]{1,0:T(8,128)} %get-tuple-element.152) | copy-start | bytes 98308
  323.2 8.9 %copy-start.17 = (f32[32,256]{1,0:T(8,128)S(1)}, f32[32,256]{1,0:T(8,128)}, u32[]{:S(2)}) copy-start(f32[32,256]{1,0:T(8,128)} %get-tuple-element.153) | copy-start | bytes 98308
  323.2 9.6 %copy-start.13 = (f32[32,1024]{1,0:T(8,128)S(1)}, f32[32,1024]{1,0:T(8,128)}, u32[]{:S(2)}) copy-start(f32[32,1024]{1,0:T(8,128)} %get-tuple-element.154) | copy-start | bytes 393220
  323.2 10.2 %copy-start.12 = (f32[32,1024]{1,0:T(8,128)S(1)}, f32[32,1024]{1,0:T(8,128)}, u32[]{:S(2)}) copy-start(f32[32,1024]{1,0:T(8,128)} %get-tuple-element.155) | copy-start | bytes 393220
  323.2 10.9 %copy-start.11 = (f32[32,1024]{1,0:T(8,128)S(1)}, f32[32,1024]{1,0:T(8,128)}, u32[]{:S(2)}) copy-start(f32[32,1024]{1,0:T(8,128)} %get-tuple-element.156) | copy-start | bytes 393220
  323.2 11.5 %copy-start.10 = (f32[32,4096]{1,0:T(8,128)S(1)}, f32[32,4096]{1,0:T(8,128)}, u32[]{:S(2)}) copy-start(f32[32,4096]{1,0:T(8,128)} %get-tuple-element.157) | copy-start | bytes 1572868
  323.2 12.3 %copy-start.9 = (f32[32,4096]{1,0:T(8,128)S(1)}, f32[32,4096]{1,0:T(8,128)}, u32[]{:S(2)}) copy-start(f32[32,4096]{1,0:T(8,128)} %get-tuple-element.158) | copy-start | bytes 1572868
  323.2 13.1 %copy-start.8 = (f32[32,4096]{1,0:T(8,128)S(1)}, f32[32,4096]{1,0:T(8,128)}, u32[]{:S(2)}) copy-start(f32[32,4096]{1,0:T(8,128)} %get-tuple-element.159) | copy-start | bytes 1572868
  323.2 13.9 %copy-start.7 = (f32[32,4096]{1,0:T(8,128)S(1)}, f32[32,4096]{1,0:T(8,128)}, u32[]{:S(2)}) copy-start(f32[32,4096]{1,0:T(8,128)} %get-tuple-element.160) | copy-start | bytes 1572868
  324.2 13.7 %copy-start.6 = (f32[32,4096]{1,0:T(8,128)S(1)}, f32[32,4096]{1,0:T(8,128)}, u32[]{:S(2)}) copy-start(f32[32,4096]{1,0:T(8,128)} %get-tuple-element.161) | copy-start | bytes 1572868
  324.2 14.5 %copy-start.5 = (f32[32,4096]{1,0:T(8,128)S(1)}, f32[32,4096]{1,0:T(8,128)}, u32[]{:S(2)}) copy-start(f32[32,4096]{1,0:T(8,128)} %get-tuple-element.162) | copy-start | bytes 1572868
  325.2 14.3 %copy-start.4 = (f32[32,4096]{1,0:T(8,128)S(1)}, f32[32,4096]{1,0:T(8,128)}, u32[]{:S(2)}) copy-start(f32[32,4096]{1,0:T(8,128)} %get-tuple-element.163) | copy-start | bytes 1572868
  330.3 10.0 %copy-start.3 = (f32[32,4096]{1,0:T(8,128)S(1)}, f32[32,4096]{1,0:T(8,128)}, u32[]{:S(2)}) copy-start(f32[32,4096]{1,0:T(8,128)} %get-tuple-element.164) | copy-start | bytes 1572868
  334.7 6.4 %copy-start.2 = (f32[32,4096]{1,0:T(8,128)S(1)}, f32[32,4096]{1,0:T(8,128)}, u32[]{:S(2)}) copy-start(f32[32,4096]{1,0:T(8,128)} %get-tuple-element.165) | copy-start | bytes 1572868
Sparse Core Ops, SparseCore 0:
  26.9 95.0 all-gather.1
  202.6 98.3 reduce-scatter.1

commit v3 on v2

--- a/solution.py
+++ b/solution.py
@@ -507,28 +507,40 @@
     return [pl.BlockSpec(memory_space=pl.ANY)] * n
 
 
+class Columns:
+    def __init__(self, ref, n):
+        self.ref, self.n = ref, n
+
+    def __getitem__(self, j):
+        return self.ref[:, pl.ds(pl.multiple_of(j * self.n, self.n), self.n)]
+
+
 def spread_weights(weights, segments, cid):
-    def kernel(q, k, v, o, g, u, d, seg, front, rest, segs, fbuf, rbuf, sbuf, send, recv):
+    def kernel(q_, k_, v_, o_, g_, u_, d_, seg, front, rest, segs, fbuf, rbuf, sbuf, kv, send, recv):
         me = Place()
         peers = swap_devs(me)
         mine = me.h * 2 + me.c
+        q, o = Columns(q_, 256), Columns(o_, 256)
+        g, u, d = Columns(g_, 1024), Columns(u_, 1024), Columns(d_, 1024)
         for j in range(4):
-            fbuf[j, :, 0:256] = q[:, 256 * j:256 * j + 256].astype(bf16)
-            fbuf[j, :, 256:384] = jnp.concatenate(
-                [k[:, 64 * j:64 * j + 64], v[:, 64 * j:64 * j + 64]], axis=1).astype(bf16)
-            fbuf[j, :, 384:640] = o[:, 256 * j:256 * j + 256].astype(bf16)
+            kv[j] = jnp.concatenate([k_[:, 64 * j:64 * j + 64], v_[:, 64 * j:64 * j + 64]], axis=1)
+        sbuf[...] = jnp.broadcast_to(seg[...], (8, SEQ))
+
+        def rounded(j, fdst, rdst):
+            fdst[:, 0:256] = q[j].astype(bf16)
+            fdst[:, 256:384] = kv[j].astype(bf16)
+            fdst[:, 384:640] = o[j].astype(bf16)
             for i, w in enumerate((g, u, d)):
-                rbuf[j, :, 1024 * i:1024 * i + 1024] = w[:, 1024 * j:1024 * j + 1024].astype(bf16)
-        sbuf[...] = jnp.broadcast_to(seg[...], (8, SEQ))
+                rdst[:, 1024 * i:1024 * i + 1024] = w[j].astype(bf16)
         meet([dev for _, dev in peers])
         w = Wire(send, recv)
         arrivals = []
         for j, dev in reversed(peers):
+            rounded(j, fbuf.at[j], rbuf.at[j])
             arrivals.append(w.go(rbuf.at[j], rest.at[mine], dev))
             arrivals.append(w.go(fbuf.at[j], front.at[mine], dev))
             arrivals.append(w.go(sbuf, segs.at[mine], dev))
-        front[mine] = fbuf[mine]
-        rest[mine] = rbuf[mine]
+        rounded(mine, front.at[mine], rest.at[mine])
         segs[mine] = sbuf[...]
         for a in arrivals:
             a.wait_recv()
@@ -539,8 +551,16 @@
         out_shape=[jax.ShapeDtypeStruct((4, 32, 640), bf16), jax.ShapeDtypeStruct((4, 32, 3072), bf16),
                    jax.ShapeDtypeStruct((4, 8, SEQ), jnp.int32)],
         in_specs=vm_specs(8), out_specs=vm_specs(3),
-        scratch_shapes=[VM((4, 32, 640), bf16), VM((4, 32, 3072), bf16), VM((8, SEQ), jnp.int32)] + dma_sems(9),
+        scratch_shapes=[VM((4, 32, 640), bf16), VM((4, 32, 3072), bf16), VM((8, SEQ), jnp.int32),
+                        VM((4, 32, 128), f32)] + dma_sems(9),
         compiler_params=params(cid))(*weights, segments)
+
+
+def gain_rows(gains):
+    one = jnp.concatenate([gains[i:i + 1, :] for i in range(16)], axis=1)
+    two = jnp.concatenate([gains[16 + i:17 + i, :] for i in range(16)], axis=1)
+    small = jnp.broadcast_to(gains[32:33, :], (128, 128)).T
+    return one, two, small[0:64, 0:1], small[64:128, 0:1]
 
 
 def rope_constants():
@@ -594,16 +614,17 @@
     return v.reshape(SEQ, v.shape[-1])
 
 
-def attention_forward(x, cot, front, segs, gain_one, gain_two, gain_query, gain_key, table, cid):
-    def kernel(x, cot, front, segs, gain_one, gain_two, gain_query, gain_key, table,
+def attention_forward(x, cot, front, segs, gains, table, cid):
+    def kernel(x, cot, front, segs, gains, table,
                a_full, cot_full, n_full, front_full, qk_pre, v_rows, mixed, middle,
                shard, shard_two, a_buf, part, sibs, t, r, send, recv, lsem):
         me = Place()
+        gain_one, gain_two, gain_query, gain_key = gain_rows(gains)
 
         def norm_one(s):
             v = x[s].astype(f32)
             inverse = lax.rsqrt(jnp.mean(v * v, axis=-1, keepdims=True) + epsilon)
-            shard[s] = (v * inverse * gain_one[...]).astype(bf16)
+            shard[s] = (v * inverse * gain_one).astype(bf16)
         chunks(128, norm_one)
         meet([me.step("x", 1), me.step("x", -1), me.step("y", 1), me.step("y", -1),
               me.step("z", 1), me.step("z", -1), me.sibling()])
@@ -612,13 +633,17 @@
                    pltpu.make_async_copy(shard, a_buf.at[me.h, me.c, me.l], lsem.at[1]),
                    pltpu.make_async_copy(cot, cot_full.at[me.h, me.c, me.l], lsem.at[2])]
         gens = ag_xy_gens(w, me, front, front_full) + [ag_z_gen(w, me, shard, a_buf)]
+        ga, gb, gz = gens
         for g in gens:
             next(g)
         for c in locals_:
             c.start()
         for c in locals_:
             c.wait()
-        run(gens)
+        for g in (ga, gb, ga, gb, ga, gb, gz, ga, gb):
+            next(g)
+        run([ga, gb])
+        run([gz])
         cot_gen = ag_z_gen(w, me, cot, cot_full)
         next(cot_gen)
         keep = pltpu.make_async_copy(a_buf, a_full, lsem.at[4])
@@ -626,25 +651,25 @@
 
         def one_pack(p, _):
             allowed, cosine, sine = pack_tables(segs, p, table)
-            weights = front_full[...].reshape(D, 640)
-            qkv = dot(pack_of(a_buf, p), weights[:, 0:384]).T
+            qkv = dot(pack_of(a_buf, p), front_full[:, :, :, 0:384].reshape(D, 384)).T
             qk_pre[p] = qkv[0:320]
             value = qkv[320:384].astype(bf16)
             v_rows[p] = value
-            kn, _i = head_norm(qkv[256:320], gain_key[...])
+            kn, _i = head_norm(qkv[256:320], gain_key)
             key_rows = turn(kn, cosine, sine).T.astype(bf16)
             heads = []
             for j in range(4):
-                qn, _i = head_norm(qkv[64 * j:64 * j + 64], gain_query[...])
+                qn, _i = head_norm(qkv[64 * j:64 * j + 64], gain_query)
                 probs = pack_probs(key_rows, turn(qn, cosine, sine).astype(bf16), allowed)
                 heads.append(dot(value, probs.astype(bf16)))
             o = jnp.concatenate(heads, axis=0).T.astype(bf16)
             mixed[p] = o
-            out = dot(o, weights[:, 384:640], 1, 1).astype(bf16)
+            out = dot(o, front_full[:, :, :, 384:640].reshape(D, 256), 1, 1).astype(bf16)
             part[lax.div(p, 2), lax.rem(p, 2)] = out.reshape(2, 128, D)
             return 0
-        lax.fori_loop(0, PACKS, one_pack, 0)
+        lax.fori_loop(0, 3, one_pack, 0)
         next(cot_gen)
+        lax.fori_loop(3, PACKS, one_pack, 0)
 
         def residual(s, v):
             middle[s] = x[s].astype(f32) + v
@@ -653,7 +678,7 @@
         def norm_two(s):
             v = middle[s]
             inverse = lax.rsqrt(jnp.mean(v * v, axis=-1, keepdims=True) + epsilon)
-            shard_two[s] = (v * inverse * gain_two[...]).astype(bf16)
+            shard_two[s] = (v * inverse * gain_two).astype(bf16)
         chunks(128, norm_two)
         n_gen = ag_z_gen(w, me, shard_two, n_full)
         next(n_gen)
@@ -671,32 +696,37 @@
         out_shape=[full, full, full, jax.ShapeDtypeStruct((4, 4, 128, 640), bf16),
                    jax.ShapeDtypeStruct((PACKS, 320, SEQ), f32), jax.ShapeDtypeStruct((PACKS, HD, SEQ), bf16),
                    jax.ShapeDtypeStruct((PACKS, SEQ, 256), bf16), jax.ShapeDtypeStruct((128, D), f32)],
-        in_specs=vm_specs(9), out_specs=any_specs(3) + vm_specs(5),
+        in_specs=vm_specs(6), out_specs=any_specs(3) + vm_specs(5),
         scratch_shapes=[VM((128, D), bf16)] * 2 + [VM((2, 2, 2, 128, D), bf16)] * 2 + rs_z_scratch(D)
         + dma_sems(64) + [pltpu.SemaphoreType.DMA((5,))],
-        compiler_params=params(cid))(x, cot, front, segs, gain_one, gain_two, gain_query, gain_key, table)
+        compiler_params=params(cid))(x, cot, front, segs, gains, table)
 
 
 def sigmoid(v):
     return 1.0 / (1.0 + jnp.exp(-v))
 
 
-def feed_forward(n_full, cot_full, weights, cid):
-    def kernel(n_hbm, cot_hbm, w_hbm, grad_hbm, out_part, db_sum,
-               n, cot, w, hidden, gate_up, part, grad, sibs, t, r, send, recv, lsem, gsem):
-        me = Place()
-        loads = [pltpu.make_async_copy(n_hbm, n, lsem.at[0])]
-        loads += [pltpu.make_async_copy(w_hbm.at[:, pl.ds(1024 * i, 1024)], w.at[:, pl.ds(1024 * i, 1024)],
-                                        lsem.at[1 + i]) for i in range(3)]
-        loads.append(pltpu.make_async_copy(cot_hbm, cot, lsem.at[4]))
-        for c in loads:
-            c.start()
-        meet([me.step("z", 1), me.step("z", -1), me.sibling()])
+def feed_forward(n_full, cot_full, weights):
+    def kernel(n_hbm, cot_hbm, w_hbm, grad_hbm, hidden_hbm, gate_up_hbm,
+               n, cot, w, hidden, gate_up, grad, lsem, wsem, gsem):
+        loads = [pltpu.make_async_copy(n_hbm, n, lsem.at[0]), pltpu.make_async_copy(cot_hbm, cot, lsem.at[1])]
+        loads[0].start()
+
+        def piece(i, k):
+            here = pl.ds(pl.multiple_of(i * 256 + 1024 * k, 256), 256)
+            return pltpu.make_async_copy(w_hbm.at[:, here], w.at[:, here], wsem.at[i, k])
+        for i in range(4):
+            for k in range(3):
+                piece(i, k).start()
+            if i == 0:
+                loads[1].start()
         for c in loads:
             c.wait()
 
         def hidden_block(i, _):
             at = pl.multiple_of(i * 256, 256)
+            for k in range(3):
+                piece(i, k).wait()
             rows = n[...].reshape(ROWS, D)
             g = dot(rows, w[:, pl.ds(at, 256)])
             u = dot(rows, w[:, pl.ds(at + 1024, 256)])
@@ -708,19 +738,10 @@
             gate_up[:, pl.ds(at + 1024, 256)] = (dh * silu).astype(bf16)
             return 0
         lax.fori_loop(0, 4, hidden_block, 0)
-
-        def back_block(i, _):
-            at = pl.multiple_of(i * 256, 256)
-            v = dot(gate_up[...], w[pl.ds(at, 256), 0:2048], 1, 1).astype(bf16)
-            part[:, :, :, :, pl.ds(at, 256)] = v.reshape(2, 2, 2, 128, 256)
-            return 0
-        lax.fori_loop(0, 8, back_block, 0)
-        wire = Wire(send, recv)
-
-        def put(s, v):
-            db_sum[s] = v
-        gen = rs_z_gen(wire, me, part, put, sibs, t, r)
-        next(gen)
+        keep = [pltpu.make_async_copy(hidden, hidden_hbm, lsem.at[2]),
+                pltpu.make_async_copy(gate_up, gate_up_hbm, lsem.at[3])]
+        for c in keep:
+            c.start()
         stores = []
         for i in range(4):
             at = 512 * i
@@ -732,40 +753,82 @@
             c = pltpu.make_async_copy(grad.at[slot], grad_hbm.at[pl.ds(at, 512)], gsem.at[i])
             c.start()
             stores.append(c)
-            if i == 0 or i == 2:
-                next(gen)
+        for c in stores[2:] + keep:
+            c.wait()
+
+    full = (2, 2, 2, 128, D)
+    return pl.pallas_call(
+        kernel,
+        out_shape=[jax.ShapeDtypeStruct((D, 3072), bf16), jax.ShapeDtypeStruct((ROWS, 1024), bf16),
+                   jax.ShapeDtypeStruct((ROWS, 2048), bf16)],
+        in_specs=any_specs(3), out_specs=any_specs(3),
+        scratch_shapes=[VM(full, bf16), VM(full, bf16), VM((D, 3072), bf16), VM((ROWS, 1024), bf16),
+                        VM((ROWS, 2048), bf16), VM((2, 512, 3072), bf16), pltpu.SemaphoreType.DMA((4,)),
+                        pltpu.SemaphoreType.DMA((4, 3)), pltpu.SemaphoreType.DMA((4,))],
+        compiler_params=pltpu.CompilerParams(has_side_effects=True, vmem_limit_bytes=60 * 2**20))(
+            n_full, cot_full, weights)
+
+
+def feed_back(hidden, gate_up, weights, cid):
+    def kernel(hidden_hbm, gate_up_hbm, w_hbm, out_part, db_sum, hidden, gate_up, w, part, sibs, t, r, send, recv, lsem, wsem):
+        me = Place()
+        loads = [pltpu.make_async_copy(gate_up_hbm, gate_up, lsem.at[0]),
+                 pltpu.make_async_copy(hidden_hbm, hidden, lsem.at[1])]
+        loads[0].start()
+
+        def piece(i):
+            here = pl.ds(pl.multiple_of(i * 256, 256), 256)
+            return pltpu.make_async_copy(w_hbm.at[here], w.at[here], wsem.at[i])
+        for i in range(8):
+            piece(i).start()
+        loads[1].start()
+        meet([me.step("z", 1), me.step("z", -1), me.sibling()])
+        loads[0].wait()
+
+        def back_block(i, _):
+            at = pl.multiple_of(i * 256, 256)
+            piece(i).wait()
+            v = dot(gate_up[...], w[pl.ds(at, 256), 0:2048], 1, 1).astype(bf16)
+            part[:, :, :, :, pl.ds(at, 256)] = v.reshape(2, 2, 2, 128, 256)
+            return 0
+        lax.fori_loop(0, 8, back_block, 0)
+        wire = Wire(send, recv)
+
+        def put(s, v):
+            db_sum[s] = v
+        gen = rs_z_gen(wire, me, part, put, sibs, t, r)
+        next(gen)
+        loads[1].wait()
 
         def out_block(i, _):
             at = pl.multiple_of(i * 256, 256)
             v = dot(hidden[...], w[pl.ds(at, 256), 2048:3072], 1, 1).astype(bf16)
             out_part[:, :, :, :, pl.ds(at, 256)] = v.reshape(2, 2, 2, 128, 256)
             return 0
-        lax.fori_loop(0, 8, out_block, 0)
+        lax.fori_loop(0, 2, out_block, 0)
+        next(gen)
+        lax.fori_loop(2, 8, out_block, 0)
         run([gen])
-        stores[2].wait()
-        stores[3].wait()
         wire.finish()
 
     full = (2, 2, 2, 128, D)
     return pl.pallas_call(
         kernel,
-        out_shape=[jax.ShapeDtypeStruct((D, 3072), bf16), jax.ShapeDtypeStruct(full, bf16),
-                   jax.ShapeDtypeStruct((128, D), f32)],
-        in_specs=any_specs(3), out_specs=any_specs(1) + vm_specs(2),
-        scratch_shapes=[VM(full, bf16), VM(full, bf16), VM((D, 3072), bf16), VM((ROWS, 1024), bf16),
-                        VM((ROWS, 2048), bf16), VM(full, bf16), VM((2, 512, 3072), bf16)]
-        + rs_z_scratch(D) + dma_sems(16) + [pltpu.SemaphoreType.DMA((5,)), pltpu.SemaphoreType.DMA((4,))],
-        compiler_params=params(cid, 60))(n_full, cot_full, weights)
+        out_shape=[jax.ShapeDtypeStruct(full, bf16), jax.ShapeDtypeStruct((128, D), f32)],
+        in_specs=any_specs(3), out_specs=vm_specs(2),
+        scratch_shapes=[VM((ROWS, 1024), bf16), VM((ROWS, 2048), bf16), VM((D, 3072), bf16), VM(full, bf16)]
+        + rs_z_scratch(D) + dma_sems(16) + [pltpu.SemaphoreType.DMA((2,)), pltpu.SemaphoreType.DMA((8,))],
+        compiler_params=params(cid, 60))(hidden, gate_up, weights)
 
 
 def attention_backward(x, cot, middle, db_sum, out_part, a_full, front_full, qk_pre, v_rows, mixed, segs,
-                       gain_one, gain_two, gain_query, gain_key, table, cid):
+                       gains, table, cid):
     def kernel(x, cot, middle, db_sum, out_part, a_full, front_full, qk_pre, v_rows, mixed, segs,
-               gain_one, gain_two, gain_query, gain_key, table,
-               input_grad, block_output, front_mine, gains,
+               gains, table, input_grad, block_output, front_mine, gain_terms,
                shard, dm_full, mid_grad, dqkv, part, front_grad, q_acc, k_acc, one_acc, two_acc,
                sibs_a, t_a, r_a, sibs_b, t_b, r_b, t1, r1, t2, r2, mid, send, recv, lsem):
         me = Place()
+        gain_one, gain_two, gain_query, gain_key = gain_rows(gains)
         two_acc[...] = jnp.zeros_like(two_acc)
         one_acc[...] = jnp.zeros_like(one_acc)
         q_acc[...] = jnp.zeros_like(q_acc)
@@ -778,7 +841,7 @@
             return inverse * (scaled - z * inverse * inverse * inner), up * z * inverse
 
         def norm_two(s):
-            dz, terms = back(middle[s], gain_two[...], db_sum[s])
+            dz, terms = back(middle[s], gain_two, db_sum[s])
             v = cot[s].astype(f32) + dz
             mid_grad[s] = v
             shard[s] = v.astype(bf16)
@@ -801,11 +864,10 @@
 
         def one_pack(p, _):
             allowed, cosine, sine = pack_tables(segs, p, table)
-            weights = front_full[...].reshape(D, 640)
-            mixed_grad = dot(pack_of(dm_full, p), weights[:, 384:640]).T.astype(bf16)
+            mixed_grad = dot(pack_of(dm_full, p), front_full[:, :, :, 384:640].reshape(D, 256)).T.astype(bf16)
             value_rows = v_rows[p].astype(f32).T.astype(bf16)
             key_pre = qk_pre[p, 256:320]
-            kn, k_inverse = head_norm(key_pre, gain_key[...])
+            kn, k_inverse = head_norm(key_pre, gain_key)
             kr = turn(kn, cosine, sine)
             key_rows = kr.T.astype(bf16)
             kr = kr.astype(bf16)
@@ -815,7 +877,7 @@
             terms_q = jnp.zeros((HD, SEQ), f32)
             for j in range(4):
                 query_pre = qk_pre[p, 64 * j:64 * j + 64]
-                qn, q_inverse = head_norm(query_pre, gain_query[...])
+                qn, q_inverse = head_norm(query_pre, gain_query)
                 qr = turn(qn, cosine, sine).astype(bf16)
                 probs = pack_probs(key_rows, qr, allowed)
                 do = mixed_grad[64 * j:64 * j + 64]
@@ -825,22 +887,22 @@
                 dqr = dot(kr, ds) * score_scale
                 dk += dot(qr, ds, 1, 1)
                 dv += dot(do, probs.astype(bf16), 1, 1)
-                dq, terms = head_norm_back(query_pre, q_inverse, gain_query[...], turn_back(dqr, cosine, sine))
+                dq, terms = head_norm_back(query_pre, q_inverse, gain_query, turn_back(dqr, cosine, sine))
                 terms_q += terms
                 heads.append(dq)
-            dk, terms_k = head_norm_back(key_pre, k_inverse, gain_key[...], turn_back(dk * score_scale, cosine, sine))
+            dk, terms_k = head_norm_back(key_pre, k_inverse, gain_key, turn_back(dk * score_scale, cosine, sine))
             q_acc[...] += terms_q
             k_acc[...] += terms_k
             grads = jnp.concatenate(heads + [dk, dv], axis=0).T.astype(bf16)
             dqkv[p] = grads
-            out = dot(grads, weights[:, 0:384], 1, 1).astype(bf16)
+            out = dot(grads, front_full[:, :, :, 0:384].reshape(D, 384), 1, 1).astype(bf16)
             part[lax.div(p, 2), lax.rem(p, 2)] = out.reshape(2, 128, D)
             return 0
         lax.fori_loop(0, 2, one_pack, 0)
         next(out_gen)
         lax.fori_loop(2, PACKS, one_pack, 0)
         next(out_gen)
-        for i in range(4):
+        def grad_block(i):
             at = 512 * i
             a_rows = a_full[:, :, :, :, at:at + 512].reshape(ROWS, 512)
             dm_rows = dm_full[:, :, :, :, at:at + 512].reshape(ROWS, 512)
@@ -849,34 +911,43 @@
             front_grad[i] = g.astype(bf16).reshape(4, 128, 640)
 
         def put_in(s, v):
-            dz, terms = back(x[s].astype(f32), gain_one[...], v)
+            dz, terms = back(x[s].astype(f32), gain_one, v)
             input_grad[s] = mid_grad[s] + dz
             one_acc[...] += terms
+        in_gen = rs_z_gen(w, me, part, put_in, sibs_b, t_b, r_b)
+        next(in_gen)
+        grad_block(0)
         run([out_gen])
-        in_gen = rs_z_gen(w, me, part, put_in, sibs_b, t_b, r_b)
-        run([in_gen] + rs_xy_gens(w, me, front_grad, front_mine, t1, r1, t2, r2, mid))
+        next(in_gen)
+        for i in range(1, 4):
+            grad_block(i)
+        ga, gb = rs_xy_gens(w, me, front_grad, front_mine, t1, r1, t2, r2, mid)
+        for g in (ga, gb, ga, gb, in_gen, ga, gb, ga, gb, ga, gb):
+            next(g)
+        run([ga, gb])
+        run([in_gen])
         w.finish()
         one = jnp.sum(one_acc[...], axis=0, keepdims=True)
         two = jnp.sum(two_acc[...], axis=0, keepdims=True)
         for i in range(16):
-            gains[i:i + 1, :] = one[:, 128 * i:128 * i + 128]
-            gains[16 + i:17 + i, :] = two[:, 128 * i:128 * i + 128]
+            gain_terms[i:i + 1, :] = one[:, 128 * i:128 * i + 128]
+            gain_terms[16 + i:17 + i, :] = two[:, 128 * i:128 * i + 128]
         small = jnp.concatenate([q_acc[...], k_acc[...]], axis=0).T
-        gains[32:33, :] = jnp.sum(small, axis=0, keepdims=True)
+        gain_terms[32:33, :] = jnp.sum(small, axis=0, keepdims=True)
 
     full = (2, 2, 2, 128, D)
     rows = jax.ShapeDtypeStruct((128, D), f32)
     return pl.pallas_call(
         kernel,
         out_shape=[rows, rows, jax.ShapeDtypeStruct((128, 640), bf16), jax.ShapeDtypeStruct((33, 128), f32)],
-        in_specs=vm_specs(16), out_specs=vm_specs(4),
+        in_specs=vm_specs(13), out_specs=vm_specs(4),
         scratch_shapes=[VM((128, D), bf16), VM(full, bf16), VM((128, D), f32), VM((PACKS, SEQ, 384), bf16),
                         VM(full, bf16), VM((4, 4, 128, 640), bf16), VM((HD, SEQ), f32), VM((HD, SEQ), f32),
                         VM((16, D), f32), VM((16, D), f32)]
         + rs_z_scratch(D) * 2 + rs_xy_scratch(640) + dma_sems(64) + [pltpu.SemaphoreType.DMA((2,))],
         compiler_params=params(cid, 60))(
             x, cot, middle, db_sum, out_part, a_full, front_full, qk_pre, v_rows, mixed, segs,
-            gain_one, gain_two, gain_query, gain_key, table)
+            gains, table)
 
 
 def adam(weight, moment, square, gradient, rate, decay):
@@ -890,17 +961,9 @@
 SPANS = (256, 64, 64, 256, 1024, 1024, 1024)
 
 
-def update(front, rest, gain_terms, gain_states, states, cid):
-    def kernel(*refs):
-        front, rest, terms, g_w, g_m, g_v = refs[:6]
-        ins, g_out, outs = refs[6:27], refs[27:30], refs[30:51]
-        fbuf, rbuf, z_in, x_in, y_in = refs[51:56]
-        held, made = refs[56:77], refs[77:98]
-        send, recv, lsem, osem = refs[98:]
+def return_gradients(front, rest, gain_terms, cid):
+    def kernel(front, rest, terms, fbuf, rbuf, gain_sum, z_in, x_in, y_in, send, recv):
         me = Place()
-        loads = [pltpu.make_async_copy(a, b, lsem.at[i]) for i, (a, b) in enumerate(zip(ins, held))]
-        for c in loads:
-            c.start()
         peers = swap_devs(me)
         mine = me.h * 2 + me.c
         zs = [me.at(z=m4(me.z + dz), c=lax.rem(me.c + dc, 2)) for dz in range(4) for dc in range(2) if dz or dc]
@@ -933,18 +996,39 @@
         gs = share(total(x_in, 4), y_in, me.y, ys)
         for c in gs:
             c.wait_recv()
-        new = adam(g_w[...], g_m[...], g_v[...], total(y_in, 4), gain_rate, 0.0)
+        gain_sum[...] = total(y_in, 4)
+        for a in arrivals:
+            a.wait_recv()
+        w.finish()
+
+    return pl.pallas_call(
+        kernel, out_shape=[jax.ShapeDtypeStruct((4, 32, 640), bf16), jax.ShapeDtypeStruct((4, 32, 3072), bf16),
+                           jax.ShapeDtypeStruct((33, 128), f32)],
+        in_specs=vm_specs(3), out_specs=vm_specs(3),
+        scratch_shapes=[VM((8, 33, 128), f32), VM((4, 33, 128), f32), VM((4, 33, 128), f32)] + dma_sems(19),
+        compiler_params=params(cid))(front, rest, gain_terms)
+
+
+def update(front, rest, gain_sum, gain_states, states, tokens):
+    def kernel(*refs):
+        front, rest, g_sum, g_w, g_m, g_v = refs[:6]
+        ins, t_in, g_out, outs, t_out = refs[6:27], refs[27:29], refs[29:32], refs[32:53], refs[53:55]
+        held, made = refs[55:76], refs[76:97]
+        lsem, osem, tsem = refs[97:]
+        loads = [pltpu.make_async_copy(a, b, lsem.at[i]) for i, (a, b) in enumerate(zip(ins, held))]
+        passing = [pltpu.make_async_copy(a, b, tsem.at[i]) for i, (a, b) in enumerate(zip(t_in, t_out))]
+        for c in loads + passing:
+            c.start()
+        new = adam(g_w[...], g_m[...], g_v[...], g_sum[...], gain_rate, 0.0)
         for ref, v in zip(g_out, new):
             ref[...] = v
-        for c in loads:
-            c.wait()
-        for a in arrivals:
-            a.wait_recv()
         stores = []
         at = {False: 0, True: 0}
         for i, (n, rate) in enumerate(zip(SPANS, RATES)):
             late = i >= 4
-            buf = rbuf if late else fbuf
+            buf = rest if late else front
+            for k in range(3):
+                loads[3 * i + k].wait()
             for j in range(4):
                 here = pl.ds(n * j, n)
                 grad = buf[j, :, at[late]:at[late] + n].astype(f32)
@@ -957,19 +1041,18 @@
                 c = pltpu.make_async_copy(made[3 * i + k], outs[3 * i + k], osem.at[3 * i + k])
                 c.start()
                 stores.append(c)
-        for c in stores:
+        for c in stores + passing:
             c.wait()
-        w.finish()
 
     shapes = [jax.ShapeDtypeStruct(s.shape, f32) for s in states]
     gain_shape = jax.ShapeDtypeStruct((33, 128), f32)
     return pl.pallas_call(
-        kernel, out_shape=[gain_shape] * 3 + shapes,
-        in_specs=vm_specs(6) + any_specs(21), out_specs=vm_specs(3) + any_specs(21),
-        scratch_shapes=[VM((4, 32, 640), bf16), VM((4, 32, 3072), bf16), VM((8, 33, 128), f32), VM((4, 33, 128), f32),
-                        VM((4, 33, 128), f32)] + [VM(s.shape, f32) for s in states] * 2
-        + dma_sems(19) + [pltpu.SemaphoreType.DMA((21,)), pltpu.SemaphoreType.DMA((21,))],
-        compiler_params=params(cid))(front, rest, gain_terms, *gain_states, *states)
+        kernel, out_shape=[gain_shape] * 3 + shapes + [jax.ShapeDtypeStruct(t.shape, f32) for t in tokens],
+        in_specs=vm_specs(6) + any_specs(23), out_specs=vm_specs(3) + any_specs(23),
+        scratch_shapes=[VM(s.shape, f32) for s in states] * 2
+        + [pltpu.SemaphoreType.DMA((21,)), pltpu.SemaphoreType.DMA((21,)), pltpu.SemaphoreType.DMA((2,))],
+        compiler_params=pltpu.CompilerParams(has_side_effects=True, vmem_limit_bytes=56 * 2**20))(
+            front, rest, gain_sum, *gain_states, *states, *tokens)
 
 
 from jax.sharding import PartitionSpec as P
@@ -986,25 +1069,24 @@
 
 
 def local(block_input, output_grad, segment_ids, norm_gains, gain_moment, gain_square, *states):
-    gain_one = norm_gains[:D][None]
-    gain_two = norm_gains[D : 2 * D][None]
-    gain_query = norm_gains[2 * D : 2 * D + HD][:, None]
-    gain_key = norm_gains[2 * D + HD :][:, None]
+    square = lambda v: v.reshape(33, 128)
+    gains = square(norm_gains)
     table = jnp.asarray(rope_constants())
     front_shard, rest_shard, segments = spread_weights(states[::3], segment_ids, 1)
     rest_full = gather_plane(rest_shard.reshape(128, 3072))
     one_full, cot_full, two_full, front_full, qk_pre, v_rows, mixed, middle = attention_forward(
-        block_input, output_grad, front_shard.reshape(128, 640), segments, gain_one, gain_two, gain_query, gain_key,
-        table, 2)
-    rest_grad, out_part, db_sum = feed_forward(two_full, cot_full, rest_full, 3)
+        block_input, output_grad, front_shard.reshape(128, 640), segments, gains, table, 2)
+    rest_grad, hidden, gate_up = feed_forward(two_full, cot_full, rest_full)
     rest_mine = scatter_plane(rest_grad)
+    out_part, db_sum = feed_back(hidden, gate_up, rest_full, 3)
     input_grad, block_output, front_mine, gain_terms = attention_backward(
         block_input, output_grad, middle, db_sum, out_part, one_full, front_full, qk_pre, v_rows, mixed, segments,
-        gain_one, gain_two, gain_query, gain_key, table, 4)
-    square = lambda v: v.reshape(33, 128)
-    news = update(front_mine.reshape(4, 32, 640), rest_mine.reshape(4, 32, 3072), gain_terms,
-                  [square(norm_gains), square(gain_moment), square(gain_square)], states, 5)
-    return (block_output, input_grad) + tuple(v.reshape(-1) for v in news[:3]) + tuple(news[3:])
+        gains, table, 4)
+    front_back, rest_back, gain_sum = return_gradients(
+        front_mine.reshape(4, 32, 640), rest_mine.reshape(4, 32, 3072), gain_terms, 5)
+    news = update(front_back, rest_back, gain_sum, [gains, square(gain_moment), square(gain_square)], states,
+                  (block_output, input_grad))
+    return tuple(news[-2:]) + tuple(v.reshape(-1) for v in news[:3]) + tuple(news[3:-2])
 
 
 def solution(mesh):

time: 350 us -> 385 us (1.10)
  Pallas kernels: 298 us -> 371 us
  local copies, waits for them, and re-layouts: 22.2 us -> 0 us
  waiting for transfers between devices: 13.8 us -> 0.08 us
    pallas_call x1 -> x3, Pallas kernels: 22 us -> 127 us  [the longest x1 67 us: update(): pl.pallas_call(kernel, out_shape=[gain_shape] * 3 + shapes + [jax.ShapeDt...]
    pallas_call x1, Pallas kernels: 58.8 us -> 36.8 us  [feed_forward(): pl.pallas_call(kernel, out_shape=[jax.ShapeDtypeStruct((D, 3072), bf16),...]
    unnamed x78 -> x0, local copies, waits for them, and re-layouts: 18.6 us -> none
    reduce_scatter x1, waiting for transfers between devices: 13.7 us -> 0.02 us  [scatter_plane(): lax.psum_scatter(whole, 'dp', axis_index_groups=PLANE, scatter_dimension=...]
    pallas_call x1, Pallas kernels: 113 us -> 104 us  [attention_forward(): pl.pallas_call(kernel, out_shape=[full, full, full, jax.ShapeDtypeStruct(...]
  transfers between devices with their start and end apart: 2 -> 2, of which waited for: 1 -> 0; matrix products, arithmetic and copies ran while one was open for 1% -> 0% of each run, Pallas kernels for 57% -> 59%
where the time goes in v3:
time: 385 us
  Pallas kernels  371 us (96%)
  between operations  14.2 us (4%)
    pallas_call x1, Pallas kernels, attention_forward(): pl.pallas_call(kernel, out_shape=[full, full, full, jax.ShapeDtypeStruct(...  104 us
    pallas_call x1, Pallas kernels, attention_backward(): pl.pallas_call(kernel, out_shape=[rows, rows, jax.ShapeDtypeStruct((128,...  82.7 us
    pallas_call x1, Pallas kernels, update(): pl.pallas_call(kernel, out_shape=[gain_shape] * 3 + shapes + [jax.ShapeDt...  67 us
    pallas_call x1, Pallas kernels, feed_back(): pl.pallas_call(kernel, out_shape=[jax.ShapeDtypeStruct(full, bf16), jax.S...  40.1 us
    pallas_call x1, Pallas kernels, feed_forward(): pl.pallas_call(kernel, out_shape=[jax.ShapeDtypeStruct((D, 3072), bf16),...  36.8 us
    pallas_call x1, Pallas kernels, return_gradients(): pl.pallas_call(kernel, out_shape=[jax.ShapeDtypeStruct((4, 32, 640), bf16...  20.3 us
    pallas_call x1, Pallas kernels, spread_weights(): pl.pallas_call(kernel, out_shape=[jax.ShapeDtypeStruct((4, 32, 640), bf16...  19.5 us
  transfers between devices with their start and end apart: 2, of which 0 were waited for; matrix products, arithmetic and copies ran while one was open for 0% of the time, Pallas kernels for 59%

profile of v3, /device:TPU:1, one launch (start us, length us, event | category | flops | bytes accessed | tf_op | source)
XLA Modules:
  0.0 384.9 jit_solution(12922223996733187787)
XLA Ops:
  7.2 0.0 all-gather.2.cloned.1.call-start
  7.2 19.5 %shard_map.467 = (bf16[4,32,640]{2,1,0:T(8,128)(2,1)}, bf16[4,32,3072]{2,1,0:T(8,128)(2,1)}, s32[4,8,256]{2,1,0:T(8,128)}) custom-call(f32[32,1024]{1,0:T(8,128)} %refs_6_.1, f32[32,256]{1,0:T(8,128)} %refs_9_.1, f32[32,256]{1,0:T(8,128)} %refs_12_.1, f32[32,1024]{1,0:T(8,128)} %refs_15_.1, f32[32,4096]{1,0:T(8,128)} %refs_18_.1, f32[32,4096]{1,0:T(8,128)} %refs_21_.1, ...), custom_call_target="tpu_custom_call" | custom-call | tf_op jit(solution)/shard_map/pallas_call | solution.py:549
  26.7 0.0 all-gather.2.cloned.1.call-update
  26.8 0.0 reduce-scatter.2.cloned.1.call-start
  26.8 104.2 %shard_map.468 = (bf16[2,2,2,128,2048]{4,3,2,1,0:T(8,128)(2,1)}, bf16[2,2,2,128,2048]{4,3,2,1,0:T(8,128)(2,1)}, bf16[2,2,2,128,2048]{4,3,2,1,0:T(8,128)(2,1)}, b...) custom-call(bf16[128,2048]{1,0:T(8,128)(2,1)} %x.3, ...), custom_call_target="tpu_custom_call" | custom-call | tf_op jit(solution)/shard_map/pallas_call | solution.py:694
  131.1 0.0 all-gather.2.cloned.1.call-done.w_hbm
  131.1 36.8 %shard_map.469 = (bf16[2048,3072]{1,0:T(8,128)(2,1)}, bf16[1024,1024]{1,0:T(8,128)(2,1)}, bf16[1024,2048]{1,0:T(8,128)(2,1)}) custom-call(bf16[2,2,2,128,2048]{4,3,2,1,0:T(8,128)(2,1)} %get-tuple-element.78.n_hbm, bf16[2,2,2,128,2048]{4,3,2,1,0:T(8,128)(2,1)} %get-tuple-element.79.cot_hbm, bf16[2048,3072]{1,0:T(8,128)(2,1)} %all-gather.2.cloned.1.call-done.w_hbm), custom_call_target="tpu_custom_call" | custom-call | tf_op jit(solution)/shard_map/pallas_call | solution.py:760
  167.9 0.0 reduce-scatter.2.cloned.1.call-update
  167.9 40.1 %shard_map.470 = (bf16[2,2,2,128,2048]{4,3,2,1,0:T(8,128)(2,1)}, f32[128,2048]{1,0:T(8,128)}) custom-call(bf16[1024,1024]{1,0:T(8,128)(2,1)} %get-tuple-element.81.hidden_hbm, bf16[1024,2048]{1,0:T(8,128)(2,1)} %get-tuple-element.82.gate_up_hbm, bf16[2048,3072]{1,0:T(8,128)(2,1)} %all-gather.2.cloned.1.call-done.w_hbm), custom_call_target="tpu_custom_call" | custom-call | tf_op jit(solution)/shard_map/pallas_call | solution.py:815
  208.0 82.7 %shard_map.471 = (f32[128,2048]{1,0:T(8,128)}, f32[128,2048]{1,0:T(8,128)}, bf16[128,640]{1,0:T(8,128)(2,1)}, f32[33,128]{1,0:T(8,128)}) custom-call(bf16[128,2048]{1,0:T(8,128)(2,1)} %x.3, bf16[128,2048]{1,0:T(8,128)(2,1)} %cot.3, f32[128,2048]{1,0:T(8,128)} %get-tuple-element.77.middle, f32[128,2048]{1,0:T(8,128)} %get-tuple-element.83.db_sum, ...), custom_call_target="tpu_custom_call" | custom-call | tf_op jit(solution)/shard_map/pallas_call | solution.py:940
  290.7 0.0 reduce-scatter.2.cloned.1.call-done
  290.7 20.3 %shard_map.472 = (bf16[4,32,640]{2,1,0:T(8,128)(2,1)}, bf16[4,32,3072]{2,1,0:T(8,128)(2,1)}, f32[33,128]{1,0:T(8,128)}) custom-call(bf16[4,32,640]{2,1,0:T(8,128)(2,1)} %bitcast.15, bf16[4,32,3072]{2,1,0:T(8,128)(2,1)} %bitcast.11, f32[33,128]{1,0:T(8,128)} %get-tuple-element.92.terms), custom_call_target="tpu_custom_call" | custom-call | tf_op jit(solution)/shard_map/pallas_call | solution.py:1004
  311.0 67.0 %shard_map.473 = (f32[33,128]{1,0:T(8,128)}, f32[33,128]{1,0:T(8,128)}, f32[33,128]{1,0:T(8,128)}, f32[32,1024]{1,0:T(8,128)}, f32[32,1024]{1,0:T(8,128)}, /*ind...) custom-call(bf16[4,32,640]{2,1,0:T(8,128)(2,1)} %get-tuple-element.9, ...), custom_call_target="tpu_custom_call" | custom-call | tf_op jit(solution)/shard_map/pallas_call | solution.py:1049
Async XLA Ops:
  7.2 123.9 %all-gather.2.cloned.1.call-start = ((), (), s32[]{:S(2)}) async-start(), calls=%async_computation.1 | async-start | bytes 13369344 | tf_op jit(solution)/shard_map/all_gather | solution.py:1064
  26.8 263.9 %reduce-scatter.2.cloned.1.call-start = ((), (), s32[]{:S(2)}) async-start(), calls=%async_computation.2 | async-start | bytes 13369344 | tf_op jit(solution)/shard_map/reduce_scatter | solution.py:1068
Sparse Core Ops, SparseCore 0:
  26.9 98.9 all-gather.1
  168.0 92.0 reduce-scatter.1
